TPU v7x, 32 devices: a whole 2x2x4 slice. The times are simulated.
32 devices in a mesh: row: 4 (over y, x), col: 8 (over z, core).
Axes of the slice: x: 2, y: 2, z: 4, core: 2. Of those that a mesh axis runs over, the one named last changes fastest.
Arguments:
- matrix: float32 [4096, 4096], P('row', 'col'), may hold values from -8 to 48
- pivots: int32 [2, 128], replicated, may hold values from 256 to 4095, as said below
- lower_inverse: float32 [2, 128, 128], replicated, may hold values from -1 to 1, as said below
Outputs:
- factored: float32 [4096, 4096], P('row', 'col')
Inputs may be any that keep to these rules, and one draw needn't show every extreme that they name: pivots[k, j] is the global row that panel k exchanges with global row k * 128 + j; all 256 entries are distinct. Each lower_inverse[k] is unit lower triangular.
All inputs are finite; a program needn't handle non-finite values.
Results may differ from a plain program's by a relative error of at most 0.0001.
Values sent between devices are 32-bit elements; how exact they have to be, the bound alone decides.
A program may use at most 64 MiB of HBM per device.

v0:
```python
import functools

import jax
import jax.numpy as jnp
from jax import lax
from jax.experimental import pallas as pl
from jax.experimental.pallas import tpu as pltpu
from jax.sharding import PartitionSpec as P

MESH = pl.DeviceIdType.MESH
F32 = jnp.float32
BF16 = jnp.bfloat16
CHUNKS = 16
EARLY = 3
TILES = 4


def mm(left, right):
    return jnp.dot(left, right, preferred_element_type=F32)


def exact(left, right):
    return jnp.dot(left, right, precision=lax.Precision.HIGHEST, preferred_element_type=F32)


def halves(value):
    high = value.astype(BF16)
    return high, (value - high.astype(F32)).astype(BF16)


def thirds(value):
    high = value.astype(BF16)
    rest = value - high.astype(F32)
    middle = rest.astype(BF16)
    return high, middle, (rest - middle.astype(F32)).astype(BF16)


def select(chosen, value):
    high, middle, low = thirds(value)
    return mm(chosen, high) + (mm(chosen, middle) + mm(chosen, low))


def dot3(left, right):
    left_high, left_low = left
    right_high, right_low = right
    return mm(left_high, right_high) + (mm(left_low, right_high) + mm(left_high, right_low))


def upper_inverse(upper, rows, cols):
    on_diag = rows == cols
    eye = jnp.where(on_diag, 1.0, 0.0)
    kept = jnp.where(on_diag, upper, 0.0)
    scaled = upper / jnp.sum(kept, axis=1, keepdims=True)
    power = jnp.where(rows < cols, -scaled, 0.0)
    result = eye + power
    reach = 2
    while reach < upper.shape[0]:
        power = exact(power, power)
        result = result + exact(result, power)
        reach = reach * 2
    return result / jnp.sum(kept, axis=0, keepdims=True)


def kernel(R, C, nb, a_hbm, piv_hbm, linv_hbm, asw,
           a_v, piv_ref, linv_ref, sel, sel_t, pm, pf, rsbuf, tops, tp, dpart, dbuf, dh, pan, res,
           u_hi, u_lo, u_f, hit,
           load_sem, piv_sem, linv_sem, d_s, d_r, tp_s, tp_r, rs_s, rs_r, ag_s, ag_r,
           to_s, to_r, ch_s, ch_r, sb_s, sb_r):
    height, width = a_v.shape
    two = 2 * nb
    ch = two // R
    ck = height // CHUNKS
    r = lax.axis_index("row")
    c = lax.axis_index("col")
    s = lax.rem(c, 2)
    sibling = {"col": c + 1 - 2 * s}

    load = pltpu.make_async_copy(a_hbm, a_v, load_sem)
    load_piv = pltpu.make_async_copy(piv_hbm, piv_ref, piv_sem)
    load_linv = pltpu.make_async_copy(linv_hbm, linv_ref, linv_sem)
    load_piv.start()
    load.start()
    load_linv.start()

    barrier = pltpu.get_barrier_semaphore()
    for off in range(1, R):
        pl.semaphore_signal(barrier, inc=1, device_id={"row": lax.rem(r + off, R)}, device_id_type=MESH)
    has_after = c + 2 < C
    has_before = c >= 2

    @pl.when(has_after)
    def _():
        pl.semaphore_signal(barrier, inc=1, device_id={"col": jnp.minimum(c + 2, C - 1)}, device_id_type=MESH)

    @pl.when(has_before)
    def _():
        pl.semaphore_signal(barrier, inc=1, device_id={"col": jnp.maximum(c - 2, 0)}, device_id_type=MESH)

    pl.semaphore_signal(barrier, inc=1, device_id=sibling, device_id_type=MESH)

    load_piv.wait()
    shift = nb.bit_length() - 1
    rshift = R.bit_length() - 1
    lane = lax.broadcasted_iota(jnp.int32, (nb, nb), 1)
    sub = lax.broadcasted_iota(jnp.int32, (nb, nb), 0)
    for k in range(2):
        p = piv_ref[k:k + 1, :]
        block = jnp.right_shift(p, shift)
        local = jnp.left_shift(jnp.right_shift(block, rshift), shift) + jnp.bitwise_and(p, nb - 1)
        local = jnp.where(jnp.bitwise_and(block, R - 1) == r, local, -1)
        wide = jnp.broadcast_to(local, (nb, nb))
        tall = wide.astype(F32).T
        for t in range(height // nb):
            spots = slice(t * nb, (t + 1) * nb)
            sel[spots, k * nb:(k + 1) * nb] = jnp.where(wide == sub + t * nb, 1.0, 0.0).astype(BF16)
            sel_t[k * nb:(k + 1) * nb, spots] = jnp.where(
                tall == (lane + t * nb).astype(F32), 1.0, 0.0).astype(BF16)

    load.wait()
    load_linv.wait()
    pl.semaphore_wait(barrier, R + jnp.minimum(c // 2, 1) + jnp.minimum((C - 1 - c) // 2, 1))

    def remote(src, dst, send, recv, where):
        return pltpu.make_async_remote_copy(
            src_ref=src, dst_ref=dst, send_sem=send, recv_sem=recv, device_id=where, device_id_type=MESH)

    def row_peer(off):
        return {"row": lax.rem(r + off, R)}

    def tp_copy(off):
        q = jnp.minimum(r, 1)
        return remote(a_v.at[0:nb, 0:nb], tp.at[pl.ds(pl.multiple_of(q * nb, nb), nb)],
                      tp_s.at[off - 1], tp_r.at[q], row_peer(off))

    def tops_copy(off):
        q = jnp.minimum(r, 1)
        return remote(a_v.at[0:nb], tops.at[pl.ds(pl.multiple_of(q * nb, nb), nb)],
                      to_s.at[off - 1], to_r.at[q], row_peer(off))

    def d_copy(off):
        return remote(dpart, dbuf.at[off - 1], d_s.at[off - 1], d_r.at[off - 1], row_peer(off))

    def rs_copy(off):
        to = lax.rem(r + off, R)
        return remote(pm.at[pl.ds(pl.multiple_of(to * ch, ch), ch)], rsbuf.at[off - 1],
                      rs_s.at[off - 1], rs_r.at[off - 1], {"row": to})

    def ag_copy(off):
        mine = pf.at[pl.ds(pl.multiple_of(r * ch, ch), ch)]
        return remote(mine, mine, ag_s.at[off - 1], ag_r.at[off - 1], row_peer(off))

    def ag_in(off):
        src = lax.rem(r - off + R, R)
        there = pf.at[pl.ds(pl.multiple_of(src * ch, ch), ch)]
        return remote(there, there, ag_s.at[off - 1], ag_r.at[off - 1], row_peer(off))

    def piece(side, k):
        if k < CHUNKS:
            return pan.at[side, pl.ds(k * ck, ck)]
        return dh.at[side, pl.ds((k - CHUNKS) * nb, nb)]

    def chain_copy(k):
        part = piece(s, k)
        return remote(part, part, ch_s.at[k], ch_r.at[k], {"col": jnp.minimum(c + 2, C - 2 + s)})

    def sib_copy(k):
        part = piece(s, k)
        return remote(part, part, sb_s.at[k], sb_r.at[k], sibling)

    def sib_in(k):
        part = piece(1 - s, k)
        return remote(part, part, sb_s.at[k], sb_r.at[k], sibling)

    is_top = r < 2
    at_root = c < 2

    @pl.when(at_root)
    def _():
        @pl.when(is_top)
        def _():
            for off in range(1, R):
                tp_copy(off).start()
            tp[pl.ds(pl.multiple_of(jnp.minimum(r, 1) * nb, nb), nb), :] = a_v[0:nb, 0:nb]

        dpart[...] = select(sel_t[...], a_v[:, 0:nb])
        for off in range(1, R):
            d_copy(off).start()

    ones = jnp.full((two, nb), 1.0, BF16)

    @pl.loop(0, TILES)
    def _(t):
        spots = pl.ds(pl.multiple_of(t * (height // TILES), height // TILES), height // TILES)
        hit[spots, :] = mm(sel[spots, :], ones)

    def panel(first, last):
        high, middle, low = thirds(tp[...])
        for k in range(first, last):
            spots = slice(k * ck, (k + 1) * ck)
            chosen = sel[spots, :]
            placed = mm(chosen, high) + (mm(chosen, middle) + mm(chosen, low))
            pan[s, spots, :] = jnp.where(hit[spots, :] > 0.5, placed, a_v[spots, 0:nb])
            chain_copy(k).start()
            sib_copy(k).start()

    @pl.loop(0, width // nb)
    def _(t):
        spots = pl.ds(pl.multiple_of(t * nb, nb), nb)
        pm[:, spots] = select(sel_t[...], a_v[:, spots])

    @pl.when(at_root)
    def _():
        for q in range(2):
            @pl.when(r != q)
            def _():
                part = tp.at[q * nb:(q + 1) * nb]
                remote(part, part, tp_s.at[0], tp_r.at[q], row_peer(1)).wait_recv()
        panel(0, EARLY)

    for off in range(1, R):
        rs_copy(off).start()

    @pl.when(is_top)
    def _():
        for off in range(1, R):
            tops_copy(off).start()
        tops[pl.ds(pl.multiple_of(jnp.minimum(r, 1) * nb, nb), nb), :] = a_v[0:nb, :]

    @pl.when(at_root)
    def _():
        total = dpart[...]
        for off in range(1, R):
            d_copy(off).wait_recv()
            total = total + dbuf[off - 1]
        dh[s] = total
        for k in range(CHUNKS, CHUNKS + 2):
            chain_copy(k).start()
            sib_copy(k).start()
        panel(EARLY, CHUNKS)

    def forward(k):
        @pl.when(c >= 2)
        def _():
            chain_copy(k).wait_recv()

            @pl.when(c + 2 < C)
            def _():
                chain_copy(k).start()
            sib_copy(k).start()

    for k in range(EARLY):
        forward(k)
    forward(CHUNKS)
    forward(CHUNKS + 1)

    own = pl.ds(pl.multiple_of(r * ch, ch), ch)
    total = pm[own, :]
    for off in range(1, R):
        rs_copy(off).wait_recv()
        total = total + rsbuf[off - 1]
    pf[own, :] = total
    for off in range(1, R):
        ag_copy(off).start()

    left = list(range(EARLY, CHUNKS))

    def some(count):
        for _ in range(min(count, len(left))):
            forward(left.pop(0))

    sib_in(CHUNKS).wait_recv()
    sib_in(CHUNKS + 1).wait_recv()
    upper00 = jnp.where(sub <= lane, exact(linv_ref[0], dh[0, 0:nb, :]), 0.0)
    res[0] = upper_inverse(upper00, sub, lane)
    some(1)
    res[1] = exact(dh[0, nb:two, :], res[0])
    upper01 = exact(linv_ref[0], dh[1, 0:nb, :])
    rest = dh[1, nb:two, :] - exact(res[1], upper01)
    upper11 = jnp.where(sub <= lane, exact(linv_ref[1], rest), 0.0)
    res[2] = -exact(res[0], upper01)
    some(1)
    res[3] = upper_inverse(upper11, sub, lane)
    some(2)
    res[2] = exact(res[2], res[3])
    mixed = -exact(exact(linv_ref[1], res[1]), linv_ref[0])
    some(1)

    for q in range(2):
        @pl.when(r != q)
        def _():
            part = tops.at[q * nb:(q + 1) * nb]
            remote(part, part, to_s.at[0], to_r.at[q], row_peer(1)).wait_recv()

    for t in range(width // nb):
        spots = slice(t * nb, (t + 1) * nb)
        placed = select(sel[...], tops[:, spots])
        asw[:, spots] = jnp.where(hit[...] > 0.5, placed, a_v[:, spots])
        some(1)

    for off in range(1, R):
        ag_in(off).wait_recv()

    inv_low0 = linv_ref[0]
    inv_low1 = linv_ref[1]
    u_f[0:nb, :] = dot3(halves(inv_low0), halves(pf[0:nb, :]))
    u_f[nb:two, :] = (dot3(halves(mixed), halves(pf[0:nb, :]))
                      + dot3(halves(inv_low1), halves(pf[nb:two, :])))
    high, low = halves(u_f[...])
    u_hi[...] = high
    u_lo[...] = low

    step = height // TILES
    inv0 = halves(res[0])
    cross = halves(res[2])
    inv1 = halves(res[3])

    def update(t, start):
        spots = pl.ds(start, step)
        left0 = halves(pan[0, spots, :])
        left1 = halves(pan[1, spots, :])
        low0 = dot3(left0, inv0)
        low1 = dot3(left0, cross) + dot3(left1, inv1)
        high, low = halves(jnp.concatenate([low0, low1], axis=1))
        asw[spots, :] = asw[spots, :] - dot3((high, low), (u_hi[...], u_lo[...]))

        @pl.when(c == 0)
        def _():
            asw[spots, 0:nb] = low0

        @pl.when(c == 1)
        def _():
            asw[spots, 0:nb] = low1

    per_tile = CHUNKS // TILES
    for t in range(TILES):
        some(1)
        while left and left[0] < (t + 1) * per_tile:
            some(1)
        for k in range(t * per_tile, (t + 1) * per_tile):
            sib_in(k).wait_recv()
        update(t, t * step)
        if t == 0:
            @pl.when(r == 0)
            def _():
                asw[0:nb, :] = u_f[0:nb, :]

                @pl.when(c == 0)
                def _():
                    asw[0:nb, 0:nb] = jnp.where(sub <= lane, u_f[0:nb, 0:nb], 0.0)

            @pl.when(r == 1)
            def _():
                asw[0:nb, :] = u_f[nb:two, :]

                @pl.when(c == 0)
                def _():
                    asw[0:nb, 0:nb] = res[1]

                @pl.when(c == 1)
                def _():
                    asw[0:nb, 0:nb] = jnp.where(sub <= lane, u_f[nb:two, 0:nb], 0.0)

    for off in range(1, R):
        rs_copy(off).wait_send()
        ag_copy(off).wait_send()

    @pl.when(is_top)
    def _():
        for off in range(1, R):
            tops_copy(off).wait_send()

        @pl.when(at_root)
        def _():
            for off in range(1, R):
                tp_copy(off).wait_send()

    for k in range(CHUNKS + 2):
        sib_copy(k).wait_send()

        @pl.when(c + 2 < C)
        def _():
            chain_copy(k).wait_send()

    @pl.when(at_root)
    def _():
        for off in range(1, R):
            d_copy(off).wait_send()


def on_device(matrix, pivots, lower_inverse):
    R = lax.axis_size("row")
    C = lax.axis_size("col")
    height, width = matrix.shape
    nb = lower_inverse.shape[1]
    two = 2 * nb
    dma = pltpu.SemaphoreType.DMA
    vm = pltpu.VMEM
    return pl.pallas_call(
        functools.partial(kernel, R, C, nb),
        out_shape=jax.ShapeDtypeStruct((height, width), F32),
        in_specs=[pl.BlockSpec(memory_space=pl.ANY)] * 3,
        out_specs=pl.BlockSpec(memory_space=pltpu.VMEM),
        scratch_shapes=[
            vm((height, width), F32), vm((2, nb), jnp.int32), vm((2, nb, nb), F32),
            vm((height, two), BF16), vm((two, height), BF16),
            vm((two, width), F32), vm((two, width), F32),
            vm((R - 1, two // R, width), F32), vm((two, width), F32),
            vm((two, nb), F32), vm((two, nb), F32), vm((R - 1, two, nb), F32),
            vm((2, two, nb), F32), vm((2, height, nb), F32), vm((4, nb, nb), F32),
            vm((two, width), BF16), vm((two, width), BF16), vm((two, width), F32),
            vm((height, nb), F32),
            dma, dma, dma, dma((R - 1,)), dma((R - 1,)), dma((R - 1,)), dma((2,)),
            dma((R - 1,)), dma((R - 1,)), dma((R - 1,)), dma((R - 1,)),
            dma((R - 1,)), dma((2,)), dma((CHUNKS + 2,)), dma((CHUNKS + 2,)),
            dma((CHUNKS + 2,)), dma((CHUNKS + 2,)),
        ],
        compiler_params=pltpu.CompilerParams(
            collective_id=0, has_side_effects=True, vmem_limit_bytes=56 * 1024 * 1024),
    )(matrix, pivots, lower_inverse)


def solution(mesh):
    return jax.shard_map(
        on_device,
        mesh=mesh,
        in_specs=(P("row", "col"), P(), P()),
        out_specs=P("row", "col"),
        check_vma=False,
    )
```

profile of v0, /device:TPU:29, one launch (start us, length us, event | category | flops | bytes accessed | tf_op | source)
XLA Modules:
  0.0 46.5 jit_solution(17943831885602585884)
XLA Ops:
  0.0 43.4 %shard_map.37 = f32[1024,512]{1,0:T(8,128)} custom-call(f32[1024,512]{1,0:T(8,128)} %a_hbm.1, s32[2,128]{1,0:T(2,128)} %piv_hbm.1, f32[2,128,128]{2,1,0:T(8,128)} %linv_hbm.1), custom_call_target="tpu_custom_call" | custom-call | tf_op jit(solution)/shard_map/pallas_call | solution.py:398
  43.4 3.1 %copy.5 = f32[1024,512]{1,0:T(8,128)} copy(f32[1024,512]{1,0:T(8,128)} %shard_map.37) | data formatting | bytes 4194304
where the time goes:
time: 46.7 us; the launch traced here: 46.5 us
  Pallas kernels  43.4 us (93%)
  local copies, waits for them, and re-layouts  3.08 us (7%)
    pallas_call x1, Pallas kernels, on_device(): pl.pallas_call(functools.partial(kernel, R, C, nb), out_shape=jax.ShapeDt...  43.4 us
    unnamed x1, local copies, waits for them, and re-layouts  3.08 us

commit v1 on v0

--- a/solution.py
+++ b/solution.py
@@ -12,6 +12,8 @@
 BF16 = jnp.bfloat16
 CHUNKS = 16
 EARLY = 3
+MIDDLE = 9
+ANY_EARLY = 3
 TILES = 4
 
 
@@ -61,7 +63,545 @@
     return result / jnp.sum(kept, axis=0, keepdims=True)
 
 
-def kernel(R, C, nb, a_hbm, piv_hbm, linv_hbm, asw,
+def room(R, nb):
+    return (nb // R + 31) // 16 * 16
+
+
+def kernel(R, C, nb, a_hbm, piv_ref, linv_ref, asw,
+           sel, sel_t, place, split, tcomp, pall, dall, tops, tpan, dh, pan, res, lt_hi, lt_lo,
+           me_hi, me_lo, u_hi, u_lo, u_f, hit,
+           load_sem, tq_s, tq_r, da_s, da_r, to_s, to_r,
+           ag_s, ag_r, ch_s, ch_r, sb_s, sb_r):
+    height, width = asw.shape
+    two = 2 * nb
+    cap = room(R, nb)
+    W = 2 * cap
+    ck = height // CHUNKS
+    NJ = width // nb
+    r = lax.axis_index("row")
+    c = lax.axis_index("col")
+    s = lax.rem(c, 2)
+    sibling = {"col": c + 1 - 2 * s}
+    top_half = jnp.minimum(r, 1)
+    odd = lax.rem(r, 2)
+    relay = R == 4
+
+    def flip(bit):
+        if bit == 1:
+            return r + 1 - 2 * odd
+        if bit == 2:
+            return lax.rem(r + 2, 4)
+        return 3 - r
+
+    def cols(j):
+        return pl.ds(j * nb, nb)
+
+    def load(j):
+        return pltpu.make_async_copy(a_hbm.at[:, cols(j)], asw.at[:, cols(j)], load_sem.at[j])
+
+    for j in range(NJ):
+        load(j).start()
+
+    has_after = c + 2 < C
+    has_before = c >= 2
+    at_root = c < 2
+    is_top = r < 2
+
+    barrier = pltpu.get_barrier_semaphore()
+    for off in range(1, R):
+        pl.semaphore_signal(barrier, inc=1, device_id={"row": lax.rem(r + off, R)}, device_id_type=MESH)
+
+    @pl.when(has_after)
+    def _():
+        pl.semaphore_signal(barrier, inc=1, device_id={"col": jnp.minimum(c + 2, C - 1)}, device_id_type=MESH)
+
+    @pl.when(has_before)
+    def _():
+        pl.semaphore_signal(barrier, inc=1, device_id={"col": jnp.maximum(c - 2, 0)}, device_id_type=MESH)
+
+    pl.semaphore_signal(barrier, inc=1, device_id=sibling, device_id_type=MESH)
+
+    shift = nb.bit_length() - 1
+    rshift = R.bit_length() - 1
+    lane = lax.broadcasted_iota(jnp.int32, (nb, nb), 1)
+    sub = lax.broadcasted_iota(jnp.int32, (nb, nb), 0)
+    lane_f = lane.astype(F32)
+    sub_f = sub.astype(F32)
+    before = jnp.where(sub < lane, 1.0, 0.0).astype(BF16)
+    owners, slots, talls = [], [], []
+    for k in range(2):
+        p = piv_ref[k:k + 1, :]
+        block = jnp.right_shift(p, shift)
+        owner = jnp.bitwise_and(block, R - 1)
+        local = jnp.left_shift(jnp.right_shift(block, rshift), shift) + jnp.bitwise_and(p, nb - 1)
+        hot = jnp.where(jnp.broadcast_to(owner, (16, nb)) == sub[0:16], 1.0, 0.0)
+        rank = mm(hot.astype(BF16), before)
+        slot = jnp.sum(hot * rank, axis=0, keepdims=True)
+        mine = jnp.where(owner == r, slot, -1.0)
+        match = jnp.broadcast_to(mine, (cap, nb)) == sub_f[0:cap]
+        value = jnp.broadcast_to(local.astype(F32) + 1.0, (cap, nb))
+        spot = jnp.sum(jnp.where(match, value, 0.0), axis=1, keepdims=True) - 1.0
+        owners.append(owner)
+        slots.append(slot)
+        talls.append(jnp.broadcast_to(spot, (cap, nb)))
+    if W < nb:
+        talls.append(jnp.full((nb - W, nb), -1.0, F32))
+    tall = jnp.concatenate(talls, axis=0)
+    for t in range(height // nb):
+        spots = slice(t * nb, (t + 1) * nb)
+        sel_t[:, spots] = jnp.where(tall[0:W] == lane_f[0:W] + float(t * nb), 1.0, 0.0).astype(BF16)
+
+    pl.semaphore_wait(barrier, R + jnp.minimum(c // 2, 1) + jnp.minimum((C - 1 - c) // 2, 1))
+
+    def remote(src, dst, send, recv, where):
+        return pltpu.make_async_remote_copy(
+            src_ref=src, dst_ref=dst, send_sem=send, recv_sem=recv, device_id=where, device_id_type=MESH)
+
+    def rows(index, count):
+        return pl.ds(pl.multiple_of(index * count, count), count)
+
+    def peer(off):
+        return lax.rem(r + off, R)
+
+    def origin(off):
+        return lax.rem(r - off + R, R)
+
+    def da_copy(off):
+        part = dall.at[s, rows(r, W)]
+        return remote(part, part, da_s.at[off - 1], da_r.at[off - 1], {"row": peer(off)})
+
+    def da_in(off):
+        part = dall.at[s, rows(origin(off), W)]
+        return remote(part, part, da_s.at[off - 1], da_r.at[off - 1], {"row": peer(off)})
+
+    def tq_copy(off):
+        return remote(tcomp.at[0, rows(peer(off), cap)], tpan.at[s, rows(top_half, cap)],
+                      tq_s.at[off - 1], tq_r.at[top_half], {"row": peer(off)})
+
+    def tz_copy(off):
+        return remote(tcomp.at[0, rows(peer(off), cap)], tops.at[0, rows(top_half, cap)],
+                      tq_s.at[off - 1], tq_r.at[top_half], {"row": peer(off)})
+
+    def to_copy(off):
+        return remote(tcomp.at[pl.ds(1, NJ - 1), rows(peer(off), cap)],
+                      tops.at[pl.ds(1, NJ - 1), rows(top_half, cap)],
+                      to_s.at[off - 1], to_r.at[top_half], {"row": peer(off)})
+
+    def tq_in(half):
+        part = tpan.at[s, pl.ds(half * cap, cap)]
+        return remote(part, part, tq_s.at[0], tq_r.at[half], {"row": peer(1)})
+
+    def tz_in(half):
+        part = tops.at[0, pl.ds(half * cap, cap)]
+        return remote(part, part, tq_s.at[0], tq_r.at[half], {"row": peer(1)})
+
+    def to_in(half):
+        part = tops.at[pl.ds(1, NJ - 1), pl.ds(half * cap, cap)]
+        return remote(part, part, to_s.at[0], to_r.at[half], {"row": peer(1)})
+
+    def from_tops(copy):
+        for half in range(2):
+            @pl.when(r != half)
+            def _():
+                copy(half).wait_recv()
+
+    def ag_copy(j, i):
+        at = j * (R - 1) + i
+        if not relay:
+            part = pall.at[j, rows(r, W)]
+            return remote(part, part, ag_s.at[at], ag_r.at[at], {"row": peer(i + 1)})
+        if i < 2:
+            part = pall.at[j, rows(r, W)]
+            return remote(part, part, ag_s.at[at], ag_r.at[at], {"row": flip(i + 1)})
+        bit = 1 + j % 2
+        part = pall.at[j, rows(flip(3 - bit), W)]
+        return remote(part, part, ag_s.at[at], ag_r.at[at], {"row": flip(bit)})
+
+    def ag_in(j, i):
+        at = j * (R - 1) + i
+        src = flip(i + 1) if relay else origin(i + 1)
+        part = pall.at[j, rows(src, W)]
+        return remote(part, part, ag_s.at[at], ag_r.at[at], {"row": peer(1)})
+
+    def ag_start(j):
+        for i in range(2 if relay else R - 1):
+            ag_copy(j, i).start()
+
+    def ag_relay_from(j):
+        return 1 - j % 2
+
+    def past_root(j, go):
+        if j == 0:
+            pl.when(has_before)(go)
+        else:
+            go()
+
+    def ag_pass(j):
+        if relay:
+            def go():
+                ag_in(j, ag_relay_from(j)).wait_recv()
+                ag_copy(j, 2).start()
+            past_root(j, go)
+
+    def ag_finish(j):
+        def go():
+            for i in range(R - 1):
+                if not (relay and i == ag_relay_from(j)):
+                    ag_in(j, i).wait_recv()
+        past_root(j, go)
+
+    TQ, DQ = CHUNKS, CHUNKS + 1
+
+    def piece(k):
+        if k < CHUNKS:
+            return pan.at[s, pl.ds(k * ck, ck)]
+        if k == TQ:
+            return tpan.at[s, pl.ds(0, W)]
+        return dall.at[s, rows(r, W)]
+
+    after = {"col": jnp.minimum(c + 2, C - 2 + s)}
+
+    def chain_copy(k):
+        return remote(piece(k), piece(k), ch_s.at[k], ch_r.at[k], after)
+
+    def root_copy(k):
+        return remote(a_hbm.at[pl.ds(k * ck, ck), cols(0)], piece(k), ch_s.at[k], ch_r.at[k], after)
+
+    def spread(k, side):
+        if k < CHUNKS:
+            return pan.at[side, pl.ds(k * ck, ck)]
+        return tpan.at[side, pl.ds(0, W)] if k == TQ else dall.at[side]
+
+    def sib_copy(k):
+        return remote(spread(k, s), spread(k, s), sb_s.at[k], sb_r.at[k], sibling)
+
+    def root_sib(k):
+        return remote(a_hbm.at[pl.ds(k * ck, ck), cols(0)], spread(k, s), sb_s.at[k], sb_r.at[k], sibling)
+
+    def sib_in(k):
+        return remote(spread(k, 1 - s), spread(k, 1 - s), sb_s.at[k], sb_r.at[k], sibling)
+
+    def forward(k):
+        @pl.when(has_before)
+        def _():
+            chain_copy(k).wait_recv()
+
+            @pl.when(has_after)
+            def _():
+                chain_copy(k).start()
+            if k == DQ:
+                for off in range(1, R):
+                    da_copy(off).start()
+            else:
+                sib_copy(k).start()
+
+    left = list(range(EARLY)) + [DQ] + list(range(EARLY, MIDDLE)) + [TQ] + list(range(MIDDLE, CHUNKS))
+
+    def some(count):
+        for _ in range(min(count, len(left))):
+            forward(left.pop(0))
+
+    def until(k):
+        while k in left:
+            some(1)
+
+    def from_root(first, last):
+        for k in range(first, last):
+            @pl.when(has_after)
+            def _():
+                root_copy(k).start()
+            root_sib(k).start()
+
+    @pl.when(at_root)
+    def _():
+        from_root(0, EARLY)
+
+    def gather(j):
+        return select(sel_t[...], asw[:, j * nb:(j + 1) * nb])
+
+    load(0).wait()
+    first = gather(0)
+
+    @pl.when(at_root)
+    def _():
+        dall[s, rows(r, W), :] = first
+
+        @pl.when(has_after)
+        def _():
+            chain_copy(DQ).start()
+        for off in range(1, R):
+            da_copy(off).start()
+        from_root(EARLY, MIDDLE)
+        pan[s] = asw[:, 0:nb]
+
+    @pl.when(has_before)
+    def _():
+        pall[0, rows(r, W), :] = first
+        ag_start(0)
+
+    def share(j):
+        load(j).wait()
+        pall[j, rows(r, W), :] = gather(j)
+        ag_start(j)
+
+    share(1)
+
+    if W < nb:
+        for j in range(NJ):
+            tops[j, W:nb, :] = jnp.zeros((nb - W, nb), F32)
+        for k in range(2):
+            tpan[k, W:nb, :] = jnp.zeros((nb - W, nb), F32)
+
+    @pl.when(is_top)
+    def _():
+        owner = jnp.where(r == 0, owners[0], owners[1])
+        slot = jnp.where(r == 0, slots[0], slots[1])
+        for q in range(R):
+            aim = jnp.where(owner == q, slot, -1.0)
+            split[q * cap:(q + 1) * cap, :] = jnp.where(
+                jnp.broadcast_to(aim, (cap, nb)) == sub_f[0:cap], 1.0, 0.0).astype(BF16)
+        tcomp[0] = select(split[...], asw[0:nb, 0:nb])
+
+        @pl.when(at_root)
+        def _():
+            tpan[s, rows(top_half, cap), :] = tcomp[0, rows(r, cap), :]
+            for off in range(1, R):
+                tq_copy(off).start()
+
+        @pl.when(has_before)
+        def _():
+            tops[0, rows(top_half, cap), :] = tcomp[0, rows(r, cap), :]
+            for off in range(1, R):
+                tz_copy(off).start()
+
+    until(DQ)
+
+    for j in range(2, NJ):
+        share(j)
+        ag_pass(j - 2)
+        some(1)
+
+    @pl.when(is_top)
+    def _():
+        for j in range(1, NJ):
+            tcomp[j] = select(split[...], asw[0:nb, j * nb:(j + 1) * nb])
+            tops[j, rows(top_half, cap), :] = tcomp[j, rows(r, cap), :]
+        for off in range(1, R):
+            to_copy(off).start()
+
+    some(1)
+
+    @pl.when(at_root)
+    def _():
+        from_tops(tq_in)
+
+        @pl.when(has_after)
+        def _():
+            chain_copy(TQ).start()
+        sib_copy(TQ).start()
+        from_root(MIDDLE, CHUNKS)
+        tops[0] = tpan[s]
+
+    wide = tall.T
+    for t in range(height // nb):
+        spots = slice(t * nb, (t + 1) * nb)
+        sel[spots, :] = jnp.where(wide == sub_f + float(t * nb), 1.0, 0.0).astype(BF16)
+    for k in range(2):
+        aim = owners[k].astype(F32) * float(W) + (slots[k] + float(k * cap))
+        aim = jnp.broadcast_to(aim, (nb, nb)).T
+        for t in range(R * W // nb):
+            place[k * nb:(k + 1) * nb, t * nb:(t + 1) * nb] = jnp.where(
+                aim == lane_f + float(t * nb), 1.0, 0.0).astype(BF16)
+    some(1)
+    for off in range(1, R):
+        da_in(off).wait_recv()
+    sib_copy(DQ).start()
+    some(1)
+    ag_pass(NJ - 2)
+    ones = jnp.full((nb, nb), 1.0, BF16)
+
+    @pl.loop(0, TILES)
+    def _(t):
+        spots = rows(t, height // TILES)
+        hit[spots, :] = mm(sel[spots, :], ones)
+
+    @pl.when(at_root)
+    def _():
+        pall[0] = dall[s]
+
+    some(1)
+    sib_in(DQ).wait_recv()
+    for k in range(2):
+        dh[k] = select(place[...], dall[k])
+    upper00 = jnp.where(sub <= lane, exact(linv_ref[0], dh[0, 0:nb, :]), 0.0)
+    some(1)
+    ag_pass(NJ - 1)
+    res[0] = upper_inverse(upper00, sub, lane)
+    some(1)
+    res[1] = exact(dh[0, nb:two, :], res[0])
+    upper01 = exact(linv_ref[0], dh[1, 0:nb, :])
+    rest = dh[1, nb:two, :] - exact(res[1], upper01)
+    upper11 = jnp.where(sub <= lane, exact(linv_ref[1], rest), 0.0)
+    res[2] = -exact(res[0], upper01)
+    some(2)
+    res[3] = upper_inverse(upper11, sub, lane)
+    some(2)
+    res[2] = exact(res[2], res[3])
+    mixed = -exact(exact(linv_ref[1], res[1]), linv_ref[0])
+
+    def spread_left(at, value):
+        high, low = halves(value)
+        return [mm(part, place[at * nb:(at + 1) * nb, :]) for part in (high, low)]
+
+    me_hi[0:nb, :], me_lo[0:nb, :] = [v.astype(BF16) for v in spread_left(0, linv_ref[0])]
+    below = [x + y for x, y in zip(spread_left(0, mixed), spread_left(1, linv_ref[1]))]
+    me_hi[nb:two, :], me_lo[nb:two, :] = [v.astype(BF16) for v in below]
+    some(1)
+
+    inv0 = halves(res[0])
+    cross = halves(res[2])
+    inv1 = halves(res[3])
+
+    def reduce_left(first, second):
+        left0 = halves(first)
+        left1 = halves(second)
+        return dot3(left0, inv0), dot3(left0, cross) + dot3(left1, inv1)
+
+    from_tops(to_in)
+
+    @pl.when(has_before)
+    def _():
+        from_tops(tz_in)
+
+    for j in range(NJ):
+        spots = slice(j * nb, (j + 1) * nb)
+        placed = select(sel[...], tops[j])
+        asw[:, spots] = jnp.where(hit[...] > 0.5, placed, asw[:, spots])
+        some(1)
+
+    until(TQ)
+    sib_in(TQ).wait_recv()
+    low0, low1 = reduce_left(tpan[0], tpan[1])
+    high, low = halves(jnp.concatenate([low0, low1], axis=1))
+    lt_hi[...] = high
+    lt_lo[...] = low
+    some(1)
+
+    for j in range(NJ):
+        ag_finish(j)
+        spots = slice(j * nb, (j + 1) * nb)
+        value = dot3((me_hi[...], me_lo[...]), halves(pall[j]))
+        u_f[:, spots] = value
+        u_hi[:, spots], u_lo[:, spots] = halves(value)
+        some(1)
+
+    step = height // TILES
+
+    def update(t, start):
+        spots = pl.ds(start, step)
+        low0, low1 = reduce_left(pan[0, spots, :], pan[1, spots, :])
+        chosen = sel[spots, :]
+        here = hit[spots, :] > 0.5
+        moved = mm(chosen, lt_hi[...]) + mm(chosen, lt_lo[...])
+        low0 = jnp.where(here, moved[:, 0:nb], low0)
+        low1 = jnp.where(here, moved[:, nb:two], low1)
+        high, low = halves(jnp.concatenate([low0, low1], axis=1))
+        asw[spots, :] = asw[spots, :] - dot3((high, low), (u_hi[...], u_lo[...]))
+
+        @pl.when(c == 0)
+        def _():
+            asw[spots, 0:nb] = low0
+
+        @pl.when(c == 1)
+        def _():
+            asw[spots, 0:nb] = low1
+
+    per_tile = CHUNKS // TILES
+    for t in range(TILES):
+        while left and left[0] < (t + 1) * per_tile:
+            some(1)
+        for k in range(t * per_tile, (t + 1) * per_tile):
+            sib_in(k).wait_recv()
+        update(t, t * step)
+        if t == 0:
+            @pl.when(r == 0)
+            def _():
+                asw[0:nb, :] = u_f[0:nb, :]
+
+                @pl.when(c == 0)
+                def _():
+                    asw[0:nb, 0:nb] = jnp.where(sub <= lane, u_f[0:nb, 0:nb], 0.0)
+
+            @pl.when(r == 1)
+            def _():
+                asw[0:nb, :] = u_f[nb:two, :]
+
+                @pl.when(c == 0)
+                def _():
+                    asw[0:nb, 0:nb] = res[1]
+
+                @pl.when(c == 1)
+                def _():
+                    asw[0:nb, 0:nb] = jnp.where(sub <= lane, u_f[nb:two, 0:nb], 0.0)
+
+    for j in range(NJ):
+        def gone(j=j):
+            for i in range(R - 1):
+                ag_copy(j, i).wait_send()
+        past_root(j, gone)
+
+    @pl.when(is_top)
+    def _():
+        for off in range(1, R):
+            to_copy(off).wait_send()
+            tq_copy(off).wait_send()
+
+    for off in range(1, R):
+        da_copy(off).wait_send()
+
+    for k in range(CHUNKS + 2):
+        sib_copy(k).wait_send()
+
+        @pl.when(has_after)
+        def _():
+            chain_copy(k).wait_send()
+
+
+def even_device(matrix, pivots, lower_inverse):
+    R = lax.axis_size("row")
+    C = lax.axis_size("col")
+    height, width = matrix.shape
+    nb = lower_inverse.shape[1]
+    two = 2 * nb
+    nj = width // nb
+    cap = room(R, nb)
+    dma = pltpu.SemaphoreType.DMA
+    vm = pltpu.VMEM
+    return pl.pallas_call(
+        functools.partial(kernel, R, C, nb),
+        out_shape=jax.ShapeDtypeStruct((height, width), F32),
+        in_specs=[pl.BlockSpec(memory_space=pl.ANY)] + [pl.BlockSpec(memory_space=pltpu.VMEM)] * 2,
+        out_specs=pl.BlockSpec(memory_space=pltpu.VMEM),
+        scratch_shapes=[
+            vm((height, nb), BF16), vm((2 * cap, height), BF16), vm((two, 2 * cap * R), BF16),
+            vm((cap * R, nb), BF16), vm((nj, cap * R, nb), F32), vm((nj, 2 * cap * R, nb), F32),
+            vm((2, 2 * cap * R, nb), F32), vm((nj, nb, nb), F32), vm((2, nb, nb), F32),
+            vm((2, two, nb), F32), vm((2, height, nb), F32), vm((4, nb, nb), F32),
+            vm((nb, two), BF16), vm((nb, two), BF16),
+            vm((two, 2 * cap * R), BF16), vm((two, 2 * cap * R), BF16),
+            vm((two, width), BF16), vm((two, width), BF16), vm((two, width), F32),
+            vm((height, nb), F32),
+            dma((nj,)), dma((R - 1,)), dma((2,)), dma((R - 1,)), dma((R - 1,)),
+            dma((R - 1,)), dma((2,)),
+            dma((nj * (R - 1),)), dma((nj * (R - 1),)),
+            dma((CHUNKS + 2,)), dma((CHUNKS + 2,)), dma((CHUNKS + 2,)), dma((CHUNKS + 2,)),
+        ],
+        compiler_params=pltpu.CompilerParams(
+            collective_id=0, has_side_effects=True, vmem_limit_bytes=50 * 1024 * 1024),
+    )(matrix, pivots, lower_inverse)
+
+
+def any_kernel(R, C, nb, a_hbm, piv_hbm, linv_hbm, asw,
            a_v, piv_ref, linv_ref, sel, sel_t, pm, pf, rsbuf, tops, tp, dpart, dbuf, dh, pan, res,
            u_hi, u_lo, u_f, hit,
            load_sem, piv_sem, linv_sem, d_s, d_r, tp_s, tp_r, rs_s, rs_r, ag_s, ag_r,
@@ -215,7 +755,7 @@
             def _():
                 part = tp.at[q * nb:(q + 1) * nb]
                 remote(part, part, tp_s.at[0], tp_r.at[q], row_peer(1)).wait_recv()
-        panel(0, EARLY)
+        panel(0, ANY_EARLY)
 
     for off in range(1, R):
         rs_copy(off).start()
@@ -236,7 +776,7 @@
         for k in range(CHUNKS, CHUNKS + 2):
             chain_copy(k).start()
             sib_copy(k).start()
-        panel(EARLY, CHUNKS)
+        panel(ANY_EARLY, CHUNKS)
 
     def forward(k):
         @pl.when(c >= 2)
@@ -248,7 +788,7 @@
                 chain_copy(k).start()
             sib_copy(k).start()
 
-    for k in range(EARLY):
+    for k in range(ANY_EARLY):
         forward(k)
     forward(CHUNKS)
     forward(CHUNKS + 1)
@@ -262,7 +802,7 @@
     for off in range(1, R):
         ag_copy(off).start()
 
-    left = list(range(EARLY, CHUNKS))
+    left = list(range(ANY_EARLY, CHUNKS))
 
     def some(count):
         for _ in range(min(count, len(left))):
@@ -387,7 +927,7 @@
             d_copy(off).wait_send()
 
 
-def on_device(matrix, pivots, lower_inverse):
+def any_device(matrix, pivots, lower_inverse):
     R = lax.axis_size("row")
     C = lax.axis_size("col")
     height, width = matrix.shape
@@ -396,7 +936,7 @@
     dma = pltpu.SemaphoreType.DMA
     vm = pltpu.VMEM
     return pl.pallas_call(
-        functools.partial(kernel, R, C, nb),
+        functools.partial(any_kernel, R, C, nb),
         out_shape=jax.ShapeDtypeStruct((height, width), F32),
         in_specs=[pl.BlockSpec(memory_space=pl.ANY)] * 3,
         out_specs=pl.BlockSpec(memory_space=pltpu.VMEM),
@@ -415,8 +955,28 @@
             dma((CHUNKS + 2,)), dma((CHUNKS + 2,)),
         ],
         compiler_params=pltpu.CompilerParams(
-            collective_id=0, has_side_effects=True, vmem_limit_bytes=56 * 1024 * 1024),
+            collective_id=1, has_side_effects=True, vmem_limit_bytes=50 * 1024 * 1024),
     )(matrix, pivots, lower_inverse)
+
+
+def most_kernel(R, nb, piv_ref, out_ref):
+    owner = jnp.bitwise_and(jnp.right_shift(piv_ref[...], nb.bit_length() - 1), R - 1)
+    most = jnp.zeros((2, 1), F32)
+    for q in range(R):
+        most = jnp.maximum(most, jnp.sum(jnp.where(owner == q, 1.0, 0.0), axis=1, keepdims=True))
+    out_ref[0] = jnp.max(most).astype(jnp.int32)
+
+
+def on_device(matrix, pivots, lower_inverse):
+    R = lax.axis_size("row")
+    nb = lower_inverse.shape[1]
+    most = pl.pallas_call(
+        functools.partial(most_kernel, R, nb),
+        out_shape=jax.ShapeDtypeStruct((1,), jnp.int32),
+        in_specs=[pl.BlockSpec(memory_space=pltpu.VMEM)],
+        out_specs=pl.BlockSpec(memory_space=pltpu.SMEM),
+    )(pivots)
+    return lax.cond(most[0] <= room(R, nb), even_device, any_device, matrix, pivots, lower_inverse)
 
 
 def solution(mesh):

time: 46.7 us -> 39.5 us (0.85)
  the two profiles are of different devices: /device:TPU:29 before, /device:TPU:24 now
where the time goes in v1:
time: 39.5 us; the launch traced here: 39.3 us
  Pallas kernels  37.1 us (94%)
  local copies, waits for them, and re-layouts  1.32 us (3%)
  between operations  0.67 us (2%)
    pallas_call x1, Pallas kernels, even_device(): pl.pallas_call(functools.partial(kernel, R, C, nb), out_shape=jax.ShapeDt...  35.7 us
    pallas_call x1, Pallas kernels, on_device(): pl.pallas_call(functools.partial(most_kernel, R, nb), out_shape=jax.Shape...  1.32 us
    unnamed x1, local copies, waits for them, and re-layouts  1.32 us

profile of v1, /device:TPU:24, one launch (start us, length us, event | category | flops | bytes accessed | tf_op | source)
XLA Modules:
  0.0 39.3 jit_solution(1902814778404009795)
XLA Ops:
  0.0 1.3 %shard_map.43 = s32[1]{0:T(128)} custom-call(s32[2,128]{1,0:T(2,128)} %piv_ref.1), custom_call_target="tpu_custom_call" | custom-call | tf_op jit(solution)/shard_map/pallas_call | solution.py:973
  2.0 36.0 %conditional.1 = (f32[1024,512]{1,0:T(8,128)S(1)}) conditional(s32[]{:T(128)} %bitcast, (f32[1024,512]{1,0:T(8,128)}, s32[2,128]{1,0:T(2,128)}, f32[2,128,128]{2,1,0:T(8,128)}) %tuple.11, (f32[1024,512]{1,0:T(8,128)}, s32[2,128]{1,0:T(2,128)}, f32[2,128,128]{2,1,0:T(8,128)}) %tuple.11), branch_computations={%region_0.0_spmd, %region_1.0_spmd} | conditional | bytes 8 | solution.py:979
  2.0 35.7 %branch_1_fun.1 = f32[1024,512]{1,0:T(8,128)S(1)} custom-call(f32[1024,512]{1,0:T(8,128)} %get-tuple-element.32.a_hbm, s32[2,128]{1,0:T(2,128)} %get-tuple-element.24.piv_ref, f32[2,128,128]{2,1,0:T(8,128)} %get-tuple-element.34.linv_ref), custom_call_target="tpu_custom_call" | custom-call | tf_op jit(solution)/shard_map/cond/branch_1_fun/pallas_call | solution.py:580
  38.0 1.3 %copy.13 = f32[1024,512]{1,0:T(8,128)} copy(f32[1024,512]{1,0:T(8,128)S(1)} %get-tuple-element.26) | data formatting | bytes 4194304

commit v2 on v1

--- a/solution.py
+++ b/solution.py
@@ -11,9 +11,10 @@
 F32 = jnp.float32
 BF16 = jnp.bfloat16
 CHUNKS = 16
-EARLY = 3
+EARLY = 1
 MIDDLE = 9
 ANY_EARLY = 3
+FAR = 4
 TILES = 4
 
 
@@ -63,13 +64,41 @@
     return result / jnp.sum(kept, axis=0, keepdims=True)
 
 
+def select2(chosen, value):
+    high, low = halves(value)
+    return mm(chosen, high) + mm(chosen, low)
+
+
+def close(left, right):
+    left_high, left_low = halves(left)
+    right_high, right_low = halves(right)
+    return mm(jnp.concatenate([left_high, left_low, left_high], axis=1),
+              jnp.concatenate([right_high, right_high, right_low], axis=0))
+
+
+def quick_inverse(upper, rows, cols, between):
+    on_diag = rows == cols
+    eye = jnp.where(on_diag, 1.0, 0.0)
+    kept = jnp.where(on_diag, upper, 0.0)
+    scaled = upper / jnp.sum(kept, axis=1, keepdims=True)
+    power = jnp.where(rows < cols, -scaled, 0.0)
+    result = eye + power
+    reach = 2
+    while reach < upper.shape[0]:
+        power = close(power, power)
+        result = result + close(result, power)
+        reach = reach * 2
+        if reach in (8, 32):
+            between(1)
+    return result / jnp.sum(kept, axis=0, keepdims=True)
+
+
 def room(R, nb):
     return (nb // R + 31) // 16 * 16
 
 
 def kernel(R, C, nb, a_hbm, piv_ref, linv_ref, asw,
-           sel, sel_t, place, split, tcomp, pall, dall, tops, tpan, dh, pan, res, lt_hi, lt_lo,
-           me_hi, me_lo, u_hi, u_lo, u_f, hit,
+           sel, sel_t, place, split, tcomp, pall, dall, tops, tpan, dh, pan, res, lt, inv3, me3, w3, tw, u_f, hit,
            load_sem, tq_s, tq_r, da_s, da_r, to_s, to_r,
            ag_s, ag_r, ch_s, ch_r, sb_s, sb_r):
     height, width = asw.shape
@@ -120,6 +149,171 @@
         pl.semaphore_signal(barrier, inc=1, device_id={"col": jnp.maximum(c - 2, 0)}, device_id_type=MESH)
 
     pl.semaphore_signal(barrier, inc=1, device_id=sibling, device_id_type=MESH)
+
+    pl.semaphore_wait(barrier, R + jnp.minimum(c // 2, 1) + jnp.minimum((C - 1 - c) // 2, 1))
+
+    def remote(src, dst, send, recv, where):
+        return pltpu.make_async_remote_copy(
+            src_ref=src, dst_ref=dst, send_sem=send, recv_sem=recv, device_id=where, device_id_type=MESH)
+
+    def rows(index, count):
+        return pl.ds(pl.multiple_of(index * count, count), count)
+
+    def peer(off):
+        return lax.rem(r + off, R)
+
+    def origin(off):
+        return lax.rem(r - off + R, R)
+
+    def da_copy(off):
+        part = dall.at[s, rows(r, W)]
+        return remote(part, part, da_s.at[off - 1], da_r.at[off - 1], {"row": peer(off)})
+
+    def da_in(off):
+        part = dall.at[s, rows(origin(off), W)]
+        return remote(part, part, da_s.at[off - 1], da_r.at[off - 1], {"row": peer(off)})
+
+    def tq_copy(off):
+        return remote(tcomp.at[0, rows(peer(off), cap)], tpan.at[s, rows(top_half, cap)],
+                      tq_s.at[off - 1], tq_r.at[top_half], {"row": peer(off)})
+
+    def tz_copy(off):
+        return remote(tcomp.at[0, rows(peer(off), cap)], tops.at[0, rows(top_half, cap)],
+                      tq_s.at[off - 1], tq_r.at[top_half], {"row": peer(off)})
+
+    def to_copy(off):
+        return remote(tcomp.at[pl.ds(1, NJ - 1), rows(peer(off), cap)],
+                      tops.at[pl.ds(1, NJ - 1), rows(top_half, cap)],
+                      to_s.at[off - 1], to_r.at[top_half], {"row": peer(off)})
+
+    def tq_in(half):
+        part = tpan.at[s, pl.ds(half * cap, cap)]
+        return remote(part, part, tq_s.at[0], tq_r.at[half], {"row": peer(1)})
+
+    def tz_in(half):
+        part = tops.at[0, pl.ds(half * cap, cap)]
+        return remote(part, part, tq_s.at[0], tq_r.at[half], {"row": peer(1)})
+
+    def to_in(half):
+        part = tops.at[pl.ds(1, NJ - 1), pl.ds(half * cap, cap)]
+        return remote(part, part, to_s.at[0], to_r.at[half], {"row": peer(1)})
+
+    def from_tops(copy):
+        for half in range(2):
+            @pl.when(r != half)
+            def _():
+                copy(half).wait_recv()
+
+    def ag_copy(j, i):
+        at = j * (R - 1) + i
+        if not relay:
+            part = pall.at[j, rows(r, W)]
+            return remote(part, part, ag_s.at[at], ag_r.at[at], {"row": peer(i + 1)})
+        if i < 2:
+            part = pall.at[j, rows(r, W)]
+            return remote(part, part, ag_s.at[at], ag_r.at[at], {"row": flip(i + 1)})
+        bit = 1 + j % 2
+        part = pall.at[j, rows(flip(3 - bit), W)]
+        return remote(part, part, ag_s.at[at], ag_r.at[at], {"row": flip(bit)})
+
+    def ag_in(j, i):
+        at = j * (R - 1) + i
+        src = flip(i + 1) if relay else origin(i + 1)
+        part = pall.at[j, rows(src, W)]
+        return remote(part, part, ag_s.at[at], ag_r.at[at], {"row": peer(1)})
+
+    def ag_start(j):
+        for i in range(2 if relay else R - 1):
+            ag_copy(j, i).start()
+
+    def ag_relay_from(j):
+        return 1 - j % 2
+
+    def past_root(j, go):
+        if j == 0:
+            pl.when(has_before)(go)
+        else:
+            go()
+
+    def ag_pass(j):
+        if relay:
+            def go():
+                ag_in(j, ag_relay_from(j)).wait_recv()
+                ag_copy(j, 2).start()
+            past_root(j, go)
+
+    def ag_finish(j):
+        def go():
+            for i in range(R - 1):
+                if not (relay and i == ag_relay_from(j)):
+                    ag_in(j, i).wait_recv()
+        past_root(j, go)
+
+    TQ, DQ = CHUNKS, CHUNKS + 1
+
+    def piece(k):
+        if k < CHUNKS:
+            return pan.at[s, pl.ds(k * ck, ck)]
+        if k == TQ:
+            return tpan.at[s, pl.ds(0, W)]
+        return dall.at[s, rows(r, W)]
+
+    after = {"col": jnp.minimum(c + 2, C - 2 + s)}
+
+    def chain_copy(k):
+        return remote(piece(k), piece(k), ch_s.at[k], ch_r.at[k], after)
+
+    def root_copy(k):
+        return remote(a_hbm.at[pl.ds(k * ck, ck), cols(0)], piece(k), ch_s.at[k], ch_r.at[k], after)
+
+    def spread(k, side):
+        if k < CHUNKS:
+            return pan.at[side, pl.ds(k * ck, ck)]
+        return tpan.at[side, pl.ds(0, W)] if k == TQ else dall.at[side]
+
+    def sib_copy(k):
+        return remote(spread(k, s), spread(k, s), sb_s.at[k], sb_r.at[k], sibling)
+
+    def root_sib(k):
+        return remote(a_hbm.at[pl.ds(k * ck, ck), cols(0)], spread(k, s), sb_s.at[k], sb_r.at[k], sibling)
+
+    def sib_in(k):
+        return remote(spread(k, 1 - s), spread(k, 1 - s), sb_s.at[k], sb_r.at[k], sibling)
+
+    def forward(k):
+        @pl.when(has_before)
+        def _():
+            chain_copy(k).wait_recv()
+
+            @pl.when(has_after)
+            def _():
+                chain_copy(k).start()
+            if k == DQ:
+                for off in range(1, R):
+                    da_copy(off).start()
+            else:
+                sib_copy(k).start()
+
+    left = list(range(EARLY)) + [DQ] + list(range(EARLY, MIDDLE)) + [TQ] + list(range(MIDDLE, CHUNKS))
+
+    def some(count):
+        for _ in range(min(count, len(left))):
+            forward(left.pop(0))
+
+    def until(k):
+        while k in left:
+            some(1)
+
+    def from_root(first, last):
+        for k in range(first, last):
+            @pl.when(has_after)
+            def _():
+                root_copy(k).start()
+            root_sib(k).start()
+
+    @pl.when(at_root)
+    def _():
+        from_root(0, EARLY)
 
     shift = nb.bit_length() - 1
     rshift = R.bit_length() - 1
@@ -151,176 +345,8 @@
         spots = slice(t * nb, (t + 1) * nb)
         sel_t[:, spots] = jnp.where(tall[0:W] == lane_f[0:W] + float(t * nb), 1.0, 0.0).astype(BF16)
 
-    pl.semaphore_wait(barrier, R + jnp.minimum(c // 2, 1) + jnp.minimum((C - 1 - c) // 2, 1))
-
-    def remote(src, dst, send, recv, where):
-        return pltpu.make_async_remote_copy(
-            src_ref=src, dst_ref=dst, send_sem=send, recv_sem=recv, device_id=where, device_id_type=MESH)
-
-    def rows(index, count):
-        return pl.ds(pl.multiple_of(index * count, count), count)
-
-    def peer(off):
-        return lax.rem(r + off, R)
-
-    def origin(off):
-        return lax.rem(r - off + R, R)
-
-    def da_copy(off):
-        part = dall.at[s, rows(r, W)]
-        return remote(part, part, da_s.at[off - 1], da_r.at[off - 1], {"row": peer(off)})
-
-    def da_in(off):
-        part = dall.at[s, rows(origin(off), W)]
-        return remote(part, part, da_s.at[off - 1], da_r.at[off - 1], {"row": peer(off)})
-
-    def tq_copy(off):
-        return remote(tcomp.at[0, rows(peer(off), cap)], tpan.at[s, rows(top_half, cap)],
-                      tq_s.at[off - 1], tq_r.at[top_half], {"row": peer(off)})
-
-    def tz_copy(off):
-        return remote(tcomp.at[0, rows(peer(off), cap)], tops.at[0, rows(top_half, cap)],
-                      tq_s.at[off - 1], tq_r.at[top_half], {"row": peer(off)})
-
-    def to_copy(off):
-        return remote(tcomp.at[pl.ds(1, NJ - 1), rows(peer(off), cap)],
-                      tops.at[pl.ds(1, NJ - 1), rows(top_half, cap)],
-                      to_s.at[off - 1], to_r.at[top_half], {"row": peer(off)})
-
-    def tq_in(half):
-        part = tpan.at[s, pl.ds(half * cap, cap)]
-        return remote(part, part, tq_s.at[0], tq_r.at[half], {"row": peer(1)})
-
-    def tz_in(half):
-        part = tops.at[0, pl.ds(half * cap, cap)]
-        return remote(part, part, tq_s.at[0], tq_r.at[half], {"row": peer(1)})
-
-    def to_in(half):
-        part = tops.at[pl.ds(1, NJ - 1), pl.ds(half * cap, cap)]
-        return remote(part, part, to_s.at[0], to_r.at[half], {"row": peer(1)})
-
-    def from_tops(copy):
-        for half in range(2):
-            @pl.when(r != half)
-            def _():
-                copy(half).wait_recv()
-
-    def ag_copy(j, i):
-        at = j * (R - 1) + i
-        if not relay:
-            part = pall.at[j, rows(r, W)]
-            return remote(part, part, ag_s.at[at], ag_r.at[at], {"row": peer(i + 1)})
-        if i < 2:
-            part = pall.at[j, rows(r, W)]
-            return remote(part, part, ag_s.at[at], ag_r.at[at], {"row": flip(i + 1)})
-        bit = 1 + j % 2
-        part = pall.at[j, rows(flip(3 - bit), W)]
-        return remote(part, part, ag_s.at[at], ag_r.at[at], {"row": flip(bit)})
-
-    def ag_in(j, i):
-        at = j * (R - 1) + i
-        src = flip(i + 1) if relay else origin(i + 1)
-        part = pall.at[j, rows(src, W)]
-        return remote(part, part, ag_s.at[at], ag_r.at[at], {"row": peer(1)})
-
-    def ag_start(j):
-        for i in range(2 if relay else R - 1):
-            ag_copy(j, i).start()
-
-    def ag_relay_from(j):
-        return 1 - j % 2
-
-    def past_root(j, go):
-        if j == 0:
-            pl.when(has_before)(go)
-        else:
-            go()
-
-    def ag_pass(j):
-        if relay:
-            def go():
-                ag_in(j, ag_relay_from(j)).wait_recv()
-                ag_copy(j, 2).start()
-            past_root(j, go)
-
-    def ag_finish(j):
-        def go():
-            for i in range(R - 1):
-                if not (relay and i == ag_relay_from(j)):
-                    ag_in(j, i).wait_recv()
-        past_root(j, go)
-
-    TQ, DQ = CHUNKS, CHUNKS + 1
-
-    def piece(k):
-        if k < CHUNKS:
-            return pan.at[s, pl.ds(k * ck, ck)]
-        if k == TQ:
-            return tpan.at[s, pl.ds(0, W)]
-        return dall.at[s, rows(r, W)]
-
-    after = {"col": jnp.minimum(c + 2, C - 2 + s)}
-
-    def chain_copy(k):
-        return remote(piece(k), piece(k), ch_s.at[k], ch_r.at[k], after)
-
-    def root_copy(k):
-        return remote(a_hbm.at[pl.ds(k * ck, ck), cols(0)], piece(k), ch_s.at[k], ch_r.at[k], after)
-
-    def spread(k, side):
-        if k < CHUNKS:
-            return pan.at[side, pl.ds(k * ck, ck)]
-        return tpan.at[side, pl.ds(0, W)] if k == TQ else dall.at[side]
-
-    def sib_copy(k):
-        return remote(spread(k, s), spread(k, s), sb_s.at[k], sb_r.at[k], sibling)
-
-    def root_sib(k):
-        return remote(a_hbm.at[pl.ds(k * ck, ck), cols(0)], spread(k, s), sb_s.at[k], sb_r.at[k], sibling)
-
-    def sib_in(k):
-        return remote(spread(k, 1 - s), spread(k, 1 - s), sb_s.at[k], sb_r.at[k], sibling)
-
-    def forward(k):
-        @pl.when(has_before)
-        def _():
-            chain_copy(k).wait_recv()
-
-            @pl.when(has_after)
-            def _():
-                chain_copy(k).start()
-            if k == DQ:
-                for off in range(1, R):
-                    da_copy(off).start()
-            else:
-                sib_copy(k).start()
-
-    left = list(range(EARLY)) + [DQ] + list(range(EARLY, MIDDLE)) + [TQ] + list(range(MIDDLE, CHUNKS))
-
-    def some(count):
-        for _ in range(min(count, len(left))):
-            forward(left.pop(0))
-
-    def until(k):
-        while k in left:
-            some(1)
-
-    def from_root(first, last):
-        for k in range(first, last):
-            @pl.when(has_after)
-            def _():
-                root_copy(k).start()
-            root_sib(k).start()
-
-    @pl.when(at_root)
-    def _():
-        from_root(0, EARLY)
-
-    def gather(j):
-        return select(sel_t[...], asw[:, j * nb:(j + 1) * nb])
-
     load(0).wait()
-    first = gather(0)
+    first = select(sel_t[...], asw[:, 0:nb])
 
     @pl.when(at_root)
     def _():
@@ -339,191 +365,209 @@
         pall[0, rows(r, W), :] = first
         ag_start(0)
 
-    def share(j):
+    def collect(start, stop):
+        value = select2(sel_t[...], asw[:, start * nb:stop * nb])
+        for j in range(start, stop):
+            pall[j, rows(r, W), :] = value[:, (j - start) * nb:(j - start + 1) * nb]
+
+    load(1).wait()
+    collect(1, 2)
+    for j in range(2, NJ):
         load(j).wait()
-        pall[j, rows(r, W), :] = gather(j)
-        ag_start(j)
-
-    share(1)
+    for j in range(2, NJ, 2):
+        collect(j, min(j + 2, NJ))
+
+    @pl.when(c >= FAR)
+    def _():
+        for j in range(1, NJ):
+            ag_start(j)
 
     if W < nb:
         for j in range(NJ):
             tops[j, W:nb, :] = jnp.zeros((nb - W, nb), F32)
         for k in range(2):
             tpan[k, W:nb, :] = jnp.zeros((nb - W, nb), F32)
-
-    @pl.when(is_top)
-    def _():
-        owner = jnp.where(r == 0, owners[0], owners[1])
-        slot = jnp.where(r == 0, slots[0], slots[1])
-        for q in range(R):
-            aim = jnp.where(owner == q, slot, -1.0)
-            split[q * cap:(q + 1) * cap, :] = jnp.where(
-                jnp.broadcast_to(aim, (cap, nb)) == sub_f[0:cap], 1.0, 0.0).astype(BF16)
-        tcomp[0] = select(split[...], asw[0:nb, 0:nb])
-
-        @pl.when(at_root)
-        def _():
-            tpan[s, rows(top_half, cap), :] = tcomp[0, rows(r, cap), :]
-            for off in range(1, R):
-                tq_copy(off).start()
-
-        @pl.when(has_before)
-        def _():
-            tops[0, rows(top_half, cap), :] = tcomp[0, rows(r, cap), :]
-            for off in range(1, R):
-                tz_copy(off).start()
-
-    until(DQ)
-
-    for j in range(2, NJ):
-        share(j)
-        ag_pass(j - 2)
-        some(1)
-
-    @pl.when(is_top)
-    def _():
-        for j in range(1, NJ):
-            tcomp[j] = select(split[...], asw[0:nb, j * nb:(j + 1) * nb])
-            tops[j, rows(top_half, cap), :] = tcomp[j, rows(r, cap), :]
-        for off in range(1, R):
-            to_copy(off).start()
-
-    some(1)
-
-    @pl.when(at_root)
-    def _():
-        from_tops(tq_in)
-
-        @pl.when(has_after)
-        def _():
-            chain_copy(TQ).start()
-        sib_copy(TQ).start()
-        from_root(MIDDLE, CHUNKS)
-        tops[0] = tpan[s]
-
     wide = tall.T
     for t in range(height // nb):
         spots = slice(t * nb, (t + 1) * nb)
-        sel[spots, :] = jnp.where(wide == sub_f + float(t * nb), 1.0, 0.0).astype(BF16)
+        value = jnp.where(wide == sub_f + float(t * nb), 1.0, 0.0).astype(BF16)
+        sel[spots, 0:nb] = value
+        sel[spots, nb:two] = value
     for k in range(2):
         aim = owners[k].astype(F32) * float(W) + (slots[k] + float(k * cap))
         aim = jnp.broadcast_to(aim, (nb, nb)).T
         for t in range(R * W // nb):
             place[k * nb:(k + 1) * nb, t * nb:(t + 1) * nb] = jnp.where(
                 aim == lane_f + float(t * nb), 1.0, 0.0).astype(BF16)
+
+    until(DQ)
+
+    @pl.when(c < FAR)
+    def _():
+        for j in range(1, NJ):
+            ag_start(j)
+
+    @pl.when(is_top)
+    def _():
+        owner = jnp.where(r == 0, owners[0], owners[1])
+        slot = jnp.where(r == 0, slots[0], slots[1])
+        for q in range(R):
+            aim = jnp.where(owner == q, slot, -1.0)
+            aim = jnp.where(jnp.broadcast_to(aim, (cap, nb)) == sub_f[0:cap], 1.0, 0.0).astype(BF16)
+            split[q * cap:(q + 1) * cap, 0:nb] = aim
+            split[q * cap:(q + 1) * cap, nb:two] = aim
+        value = mm(split[...], jnp.concatenate(halves(asw[0:nb, :]), axis=0))
+        for j in range(NJ):
+            tcomp[j] = value[:, j * nb:(j + 1) * nb]
+        own = jnp.where(r == 0, value[0:cap, :], value[cap:2 * cap, :])
+
+        @pl.when(at_root)
+        def _():
+            tpan[s, rows(top_half, cap), :] = own[:, 0:nb]
+            for off in range(1, R):
+                tq_copy(off).start()
+
+        @pl.when(has_before)
+        def _():
+            tops[0, rows(top_half, cap), :] = own[:, 0:nb]
+            for off in range(1, R):
+                tz_copy(off).start()
+
+        for off in range(1, R):
+            to_copy(off).start()
+        for j in range(1, NJ):
+            tops[j, rows(top_half, cap), :] = own[:, j * nb:(j + 1) * nb]
+
     some(1)
-    for off in range(1, R):
-        da_in(off).wait_recv()
-    sib_copy(DQ).start()
-    some(1)
-    ag_pass(NJ - 2)
-    ones = jnp.full((nb, nb), 1.0, BF16)
+    ones = jnp.full((two, nb), 1.0, BF16)
 
     @pl.loop(0, TILES)
     def _(t):
         spots = rows(t, height // TILES)
         hit[spots, :] = mm(sel[spots, :], ones)
 
+    some(2)
+    ag_pass(0)
+    for off in range(1, R):
+        da_in(off).wait_recv()
+    sib_copy(DQ).start()
+
     @pl.when(at_root)
     def _():
+        from_tops(tq_in)
+
+        @pl.when(has_after)
+        def _():
+            chain_copy(TQ).start()
+        sib_copy(TQ).start()
+        from_root(MIDDLE, CHUNKS)
+        tops[0] = tpan[s]
         pall[0] = dall[s]
 
     some(1)
     sib_in(DQ).wait_recv()
-    for k in range(2):
-        dh[k] = select(place[...], dall[k])
+    both = select(place[...], jnp.concatenate([dall[0], dall[1]], axis=1))
+    dh[0] = both[:, 0:nb]
+    dh[1] = both[:, nb:two]
     upper00 = jnp.where(sub <= lane, exact(linv_ref[0], dh[0, 0:nb, :]), 0.0)
+    upper01 = exact(linv_ref[0], dh[1, 0:nb, :])
     some(1)
-    ag_pass(NJ - 1)
-    res[0] = upper_inverse(upper00, sub, lane)
+    ag_pass(1)
+    res[0] = quick_inverse(upper00, sub, lane, some)
     some(1)
+    ag_pass(2)
     res[1] = exact(dh[0, nb:two, :], res[0])
-    upper01 = exact(linv_ref[0], dh[1, 0:nb, :])
     rest = dh[1, nb:two, :] - exact(res[1], upper01)
     upper11 = jnp.where(sub <= lane, exact(linv_ref[1], rest), 0.0)
-    res[2] = -exact(res[0], upper01)
-    some(2)
-    res[3] = upper_inverse(upper11, sub, lane)
-    some(2)
-    res[2] = exact(res[2], res[3])
-    mixed = -exact(exact(linv_ref[1], res[1]), linv_ref[0])
-
-    def spread_left(at, value):
+    res[2] = -close(res[0], upper01)
+    mixed = -close(close(linv_ref[1], res[1]), linv_ref[0])
+    blank = jnp.zeros((nb, nb), F32)
+    high, low = halves(jnp.concatenate([
+        jnp.concatenate([linv_ref[0], blank], axis=1),
+        jnp.concatenate([mixed, linv_ref[1]], axis=1)], axis=0))
+    span = R * W
+    high = mm(high, place[...]).astype(BF16)
+    me3[:, 0:span] = high
+    me3[:, span:2 * span] = mm(low, place[...]).astype(BF16)
+    me3[:, 2 * span:3 * span] = high
+    some(1)
+    ag_pass(3)
+    res[3] = quick_inverse(upper11, sub, lane, some)
+    for j in range(4, NJ):
+        ag_pass(j)
+    some(1)
+
+    def stack(value):
         high, low = halves(value)
-        return [mm(part, place[at * nb:(at + 1) * nb, :]) for part in (high, low)]
-
-    me_hi[0:nb, :], me_lo[0:nb, :] = [v.astype(BF16) for v in spread_left(0, linv_ref[0])]
-    below = [x + y for x, y in zip(spread_left(0, mixed), spread_left(1, linv_ref[1]))]
-    me_hi[nb:two, :], me_lo[nb:two, :] = [v.astype(BF16) for v in below]
-    some(1)
-
-    inv0 = halves(res[0])
-    cross = halves(res[2])
-    inv1 = halves(res[3])
-
-    def reduce_left(first, second):
-        left0 = halves(first)
-        left1 = halves(second)
-        return dot3(left0, inv0), dot3(left0, cross) + dot3(left1, inv1)
-
-    from_tops(to_in)
-
-    @pl.when(has_before)
-    def _():
-        from_tops(tz_in)
-
-    for j in range(NJ):
-        spots = slice(j * nb, (j + 1) * nb)
-        placed = select(sel[...], tops[j])
-        asw[:, spots] = jnp.where(hit[...] > 0.5, placed, asw[:, spots])
+        return jnp.concatenate([high, high, low], axis=0)
+
+    def row_stack(value):
+        high, low = halves(value)
+        return jnp.concatenate([high, low, high], axis=1)
+
+    inverse = jnp.concatenate([
+        jnp.concatenate([res[0], close(res[2], res[3])], axis=1),
+        jnp.concatenate([blank, res[3]], axis=1)], axis=0)
+    inv3[...] = stack(inverse)
+    left3 = row_stack(inverse)
+    for j in range(0, NJ, 2):
+        ag_finish(j)
+        ag_finish(j + 1)
+        spots = slice(j * nb, (j + 2) * nb)
+        value = mm(me3[...], stack(jnp.concatenate([pall[j], pall[j + 1]], axis=1)))
+        u_f[:, spots] = value
+        w3[:, spots] = stack(mm(left3, stack(value)))
         some(1)
 
     until(TQ)
     sib_in(TQ).wait_recv()
-    low0, low1 = reduce_left(tpan[0], tpan[1])
-    high, low = halves(jnp.concatenate([low0, low1], axis=1))
-    lt_hi[...] = high
-    lt_lo[...] = low
+    from_tops(to_in)
+
+    @pl.when(has_before)
+    def _():
+        from_tops(tz_in)
+
+    tp = row_stack(jnp.concatenate([tpan[0], tpan[1]], axis=1))
+    swapped = jnp.concatenate([tops[j] for j in range(NJ)], axis=1) - mm(tp, w3[...])
+    high, low = halves(swapped)
+    tw[0:nb, :] = high
+    tw[nb:two, :] = low
+
+    @pl.when(at_root)
+    def _():
+        high, low = halves(mm(tp, inv3[...]))
+        lt[0:nb, :] = high
+        lt[nb:two, :] = low
+
     some(1)
 
-    for j in range(NJ):
-        ag_finish(j)
-        spots = slice(j * nb, (j + 1) * nb)
-        value = dot3((me_hi[...], me_lo[...]), halves(pall[j]))
-        u_f[:, spots] = value
-        u_hi[:, spots], u_lo[:, spots] = halves(value)
+    def update(start, count):
+        spots = slice(start, start + count)
+        here = hit[spots, :] > 0.5
+        kept = row_stack(jnp.concatenate([
+            jnp.where(here, 0.0, pan[0, spots, :]), jnp.where(here, 0.0, pan[1, spots, :])], axis=1))
+        change = mm(kept, w3[...])
+        moved = mm(sel[spots, :], tw[...])
+        for j in range(NJ):
+            part = slice(j * nb, (j + 1) * nb)
+            asw[spots, part] = jnp.where(here, moved[:, part], asw[spots, part]) - change[:, part]
+
+        @pl.when(at_root)
+        def _():
+            value = mm(kept, inv3[...]) + mm(sel[spots, :], lt[...])
+            asw[spots, 0:nb] = jnp.where(c == 0, value[:, 0:nb], value[:, nb:two])
+
+    step = height // TILES
+    tiles = [(t * step, step) for t in range(TILES - 1)]
+    tiles += [(height - step, step // 2), (height - step // 2, step // 2)]
+    for start, count in tiles:
+        while left and left[0] * ck < start + count:
+            some(1)
+        for k in range(start // ck, (start + count) // ck):
+            sib_in(k).wait_recv()
+        update(start, count)
         some(1)
-
-    step = height // TILES
-
-    def update(t, start):
-        spots = pl.ds(start, step)
-        low0, low1 = reduce_left(pan[0, spots, :], pan[1, spots, :])
-        chosen = sel[spots, :]
-        here = hit[spots, :] > 0.5
-        moved = mm(chosen, lt_hi[...]) + mm(chosen, lt_lo[...])
-        low0 = jnp.where(here, moved[:, 0:nb], low0)
-        low1 = jnp.where(here, moved[:, nb:two], low1)
-        high, low = halves(jnp.concatenate([low0, low1], axis=1))
-        asw[spots, :] = asw[spots, :] - dot3((high, low), (u_hi[...], u_lo[...]))
-
-        @pl.when(c == 0)
-        def _():
-            asw[spots, 0:nb] = low0
-
-        @pl.when(c == 1)
-        def _():
-            asw[spots, 0:nb] = low1
-
-    per_tile = CHUNKS // TILES
-    for t in range(TILES):
-        while left and left[0] < (t + 1) * per_tile:
-            some(1)
-        for k in range(t * per_tile, (t + 1) * per_tile):
-            sib_in(k).wait_recv()
-        update(t, t * step)
-        if t == 0:
+        if start == 0:
             @pl.when(r == 0)
             def _():
                 asw[0:nb, :] = u_f[0:nb, :]
@@ -583,13 +627,12 @@
         in_specs=[pl.BlockSpec(memory_space=pl.ANY)] + [pl.BlockSpec(memory_space=pltpu.VMEM)] * 2,
         out_specs=pl.BlockSpec(memory_space=pltpu.VMEM),
         scratch_shapes=[
-            vm((height, nb), BF16), vm((2 * cap, height), BF16), vm((two, 2 * cap * R), BF16),
-            vm((cap * R, nb), BF16), vm((nj, cap * R, nb), F32), vm((nj, 2 * cap * R, nb), F32),
+            vm((height, two), BF16), vm((2 * cap, height), BF16), vm((two, 2 * cap * R), BF16),
+            vm((cap * R, two), BF16), vm((nj, cap * R, nb), F32), vm((nj, 2 * cap * R, nb), F32),
             vm((2, 2 * cap * R, nb), F32), vm((nj, nb, nb), F32), vm((2, nb, nb), F32),
             vm((2, two, nb), F32), vm((2, height, nb), F32), vm((4, nb, nb), F32),
-            vm((nb, two), BF16), vm((nb, two), BF16),
-            vm((two, 2 * cap * R), BF16), vm((two, 2 * cap * R), BF16),
-            vm((two, width), BF16), vm((two, width), BF16), vm((two, width), F32),
+            vm((two, two), BF16), vm((3 * two, two), BF16), vm((two, 6 * cap * R), BF16),
+            vm((3 * two, width), BF16), vm((two, width), BF16), vm((two, width), F32),
             vm((height, nb), F32),
             dma((nj,)), dma((R - 1,)), dma((2,)), dma((R - 1,)), dma((R - 1,)),
             dma((R - 1,)), dma((2,)),

time: 39.5 us -> 34.4 us (0.87)
  the two profiles are of different devices: /device:TPU:24 before, /device:TPU:25 now
where the time goes in v2:
time: 34.4 us; the launch traced here: 34.3 us
  Pallas kernels  32 us (93%)
  local copies, waits for them, and re-layouts  1.32 us (4%)
  between operations  0.67 us (2%)
    pallas_call x1, Pallas kernels, even_device(): pl.pallas_call(functools.partial(kernel, R, C, nb), out_shape=jax.ShapeDt...  30.7 us
    pallas_call x1, Pallas kernels, on_device(): pl.pallas_call(functools.partial(most_kernel, R, nb), out_shape=jax.Shape...  1.32 us
    unnamed x1, local copies, waits for them, and re-layouts  1.32 us

profile of v2, /device:TPU:25, one launch (start us, length us, event | category | flops | bytes accessed | tf_op | source)
XLA Modules:
  0.0 34.3 jit_solution(8737766164703952630)
XLA Ops:
  0.0 1.3 %shard_map.43 = s32[1]{0:T(128)} custom-call(s32[2,128]{1,0:T(2,128)} %piv_ref.1), custom_call_target="tpu_custom_call" | custom-call | tf_op jit(solution)/shard_map/pallas_call | solution.py:1016
  2.0 31.0 %conditional.1 = (f32[1024,512]{1,0:T(8,128)S(1)}) conditional(s32[]{:T(128)} %bitcast, (f32[1024,512]{1,0:T(8,128)}, s32[2,128]{1,0:T(2,128)}, f32[2,128,128]{2,1,0:T(8,128)}) %tuple.11, (f32[1024,512]{1,0:T(8,128)}, s32[2,128]{1,0:T(2,128)}, f32[2,128,128]{2,1,0:T(8,128)}) %tuple.11), branch_computations={%region_0.0_spmd, %region_1.0_spmd} | conditional | bytes 8 | solution.py:1022
  2.0 30.7 %branch_1_fun.1 = f32[1024,512]{1,0:T(8,128)S(1)} custom-call(f32[1024,512]{1,0:T(8,128)} %get-tuple-element.32.a_hbm, s32[2,128]{1,0:T(2,128)} %get-tuple-element.24.piv_ref, f32[2,128,128]{2,1,0:T(8,128)} %get-tuple-element.34.linv_ref), custom_call_target="tpu_custom_call" | custom-call | tf_op jit(solution)/shard_map/cond/branch_1_fun/pallas_call | solution.py:624
  32.9 1.3 %copy.13 = f32[1024,512]{1,0:T(8,128)} copy(f32[1024,512]{1,0:T(8,128)S(1)} %get-tuple-element.26) | data formatting | bytes 4194304

commit v3 on v2

--- a/solution.py
+++ b/solution.py
@@ -12,9 +12,14 @@
 BF16 = jnp.bfloat16
 CHUNKS = 16
 EARLY = 1
-MIDDLE = 9
+MIDDLE = 12
 ANY_EARLY = 3
 FAR = 4
+INNER = (1, 2, 2, 2)
+LAST = (1, 1, 0, 2)
+PASS = 0
+LATE_TILE = 3
+BRING = 1
 TILES = 4
 
 
@@ -98,7 +103,7 @@
 
 
 def kernel(R, C, nb, a_hbm, piv_ref, linv_ref, asw,
-           sel, sel_t, place, split, tcomp, pall, dall, tops, tpan, dh, pan, res, lt, inv3, me3, w3, tw, u_f, hit,
+           sel, sel_t, place, split, tcomp, pall, dall, tops, tpan, dh, pan, res, inv3, me3, w3, tw, u_f, hit,
            load_sem, tq_s, tq_r, da_s, da_r, to_s, to_r,
            ag_s, ag_r, ch_s, ch_r, sb_s, sb_r):
     height, width = asw.shape
@@ -280,13 +285,11 @@
     def sib_in(k):
         return remote(spread(k, 1 - s), spread(k, 1 - s), sb_s.at[k], sb_r.at[k], sibling)
 
-    def forward(k):
-        @pl.when(has_before)
+    def forward(k, inner):
+        @pl.when(has_before & (has_after if inner else c + 2 >= C))
         def _():
             chain_copy(k).wait_recv()
-
-            @pl.when(has_after)
-            def _():
+            if inner:
                 chain_copy(k).start()
             if k == DQ:
                 for off in range(1, R):
@@ -294,15 +297,22 @@
             else:
                 sib_copy(k).start()
 
-    left = list(range(EARLY)) + [DQ] + list(range(EARLY, MIDDLE)) + [TQ] + list(range(MIDDLE, CHUNKS))
+    order = list(range(EARLY)) + [DQ] + list(range(EARLY, MIDDLE)) + [TQ] + list(range(MIDDLE, CHUNKS))
+    left = order[:]
+    late = order[:]
+
+    def step_on(queue, count):
+        for _ in range(min(count, len(queue))):
+            forward(queue.pop(0), queue is left)
 
     def some(count):
-        for _ in range(min(count, len(left))):
-            forward(left.pop(0))
+        step_on(left, count)
+        step_on(late, count)
 
     def until(k):
-        while k in left:
-            some(1)
+        for queue in (left, late):
+            while k in queue:
+                step_on(queue, 1)
 
     def from_root(first, last):
         for k in range(first, last):
@@ -438,7 +448,8 @@
         for j in range(1, NJ):
             tops[j, rows(top_half, cap), :] = own[:, j * nb:(j + 1) * nb]
 
-    some(1)
+    step_on(left, INNER[0])
+    step_on(late, LAST[0])
     ones = jnp.full((two, nb), 1.0, BF16)
 
     @pl.loop(0, TILES)
@@ -446,8 +457,11 @@
         spots = rows(t, height // TILES)
         hit[spots, :] = mm(sel[spots, :], ones)
 
-    some(2)
+    step_on(left, INNER[1])
+    step_on(late, LAST[1])
     ag_pass(0)
+    step_on(left, INNER[2])
+    step_on(late, LAST[2])
     for off in range(1, R):
         da_in(off).wait_recv()
     sib_copy(DQ).start()
@@ -464,21 +478,23 @@
         tops[0] = tpan[s]
         pall[0] = dall[s]
 
-    some(1)
+    step_on(left, INNER[3])
+    step_on(late, LAST[3])
     sib_in(DQ).wait_recv()
     both = select(place[...], jnp.concatenate([dall[0], dall[1]], axis=1))
     dh[0] = both[:, 0:nb]
     dh[1] = both[:, nb:two]
-    upper00 = jnp.where(sub <= lane, exact(linv_ref[0], dh[0, 0:nb, :]), 0.0)
-    upper01 = exact(linv_ref[0], dh[1, 0:nb, :])
+    upper00 = jnp.where(sub <= lane, close(linv_ref[0], dh[0, 0:nb, :]), 0.0)
+    upper01 = close(linv_ref[0], dh[1, 0:nb, :])
     some(1)
     ag_pass(1)
+    ag_pass(2)
     res[0] = quick_inverse(upper00, sub, lane, some)
     some(1)
-    ag_pass(2)
-    res[1] = exact(dh[0, nb:two, :], res[0])
-    rest = dh[1, nb:two, :] - exact(res[1], upper01)
-    upper11 = jnp.where(sub <= lane, exact(linv_ref[1], rest), 0.0)
+    ag_pass(3)
+    res[1] = close(dh[0, nb:two, :], res[0])
+    rest = dh[1, nb:two, :] - close(res[1], upper01)
+    upper11 = jnp.where(sub <= lane, close(linv_ref[1], rest), 0.0)
     res[2] = -close(res[0], upper01)
     mixed = -close(close(linv_ref[1], res[1]), linv_ref[0])
     blank = jnp.zeros((nb, nb), F32)
@@ -491,9 +507,8 @@
     me3[:, span:2 * span] = mm(low, place[...]).astype(BF16)
     me3[:, 2 * span:3 * span] = high
     some(1)
-    ag_pass(3)
     res[3] = quick_inverse(upper11, sub, lane, some)
-    for j in range(4, NJ):
+    for j in range(4 if PASS == 0 else 3, NJ):
         ag_pass(j)
     some(1)
 
@@ -519,74 +534,81 @@
         w3[:, spots] = stack(mm(left3, stack(value)))
         some(1)
 
-    until(TQ)
-    sib_in(TQ).wait_recv()
-    from_tops(to_in)
-
-    @pl.when(has_before)
-    def _():
-        from_tops(tz_in)
-
-    tp = row_stack(jnp.concatenate([tpan[0], tpan[1]], axis=1))
-    swapped = jnp.concatenate([tops[j] for j in range(NJ)], axis=1) - mm(tp, w3[...])
-    high, low = halves(swapped)
-    tw[0:nb, :] = high
-    tw[nb:two, :] = low
-
-    @pl.when(at_root)
-    def _():
-        high, low = halves(mm(tp, inv3[...]))
-        lt[0:nb, :] = high
-        lt[nb:two, :] = low
-
-    some(1)
-
     def update(start, count):
         spots = slice(start, start + count)
         here = hit[spots, :] > 0.5
         kept = row_stack(jnp.concatenate([
             jnp.where(here, 0.0, pan[0, spots, :]), jnp.where(here, 0.0, pan[1, spots, :])], axis=1))
-        change = mm(kept, w3[...])
-        moved = mm(sel[spots, :], tw[...])
-        for j in range(NJ):
-            part = slice(j * nb, (j + 1) * nb)
-            asw[spots, part] = jnp.where(here, moved[:, part], asw[spots, part]) - change[:, part]
+        asw[spots, :] = asw[spots, :] - mm(kept, w3[...])
 
         @pl.when(at_root)
         def _():
-            value = mm(kept, inv3[...]) + mm(sel[spots, :], lt[...])
-            asw[spots, 0:nb] = jnp.where(c == 0, value[:, 0:nb], value[:, nb:two])
+            value = mm(kept, inv3[...])
+            value = jnp.where(c == 0, value[:, 0:nb], value[:, nb:two])
+            asw[spots, 0:nb] = jnp.where(here, asw[spots, 0:nb], value)
+
+    def bring():
+        until(TQ)
+        sib_in(TQ).wait_recv()
+        from_tops(to_in)
+
+        @pl.when(has_before)
+        def _():
+            from_tops(tz_in)
+
+        tp = row_stack(jnp.concatenate([tpan[0], tpan[1]], axis=1))
+        moved = jnp.concatenate([tops[j] for j in range(NJ)], axis=1) - mm(tp, w3[...])
+        tw[0:nb, :], tw[nb:two, :] = halves(moved)
+
+        @pl.when(at_root)
+        def _():
+            value = mm(tp, inv3[...])
+            tw[0:nb, 0:nb], tw[nb:two, 0:nb] = halves(jnp.where(c == 0, value[:, 0:nb], value[:, nb:two]))
+
+        for t in range(TILES):
+            spots = slice(t * step, (t + 1) * step)
+            here = hit[spots, :] > 0.5
+            moved = mm(sel[spots, :], tw[...])
+            for j in range(NJ):
+                part = slice(j * nb, (j + 1) * nb)
+                asw[spots, part] = jnp.where(here, moved[:, part], asw[spots, part])
+            some(BRING)
+
+    def finish_top():
+        @pl.when(r == 0)
+        def _():
+            asw[0:nb, :] = u_f[0:nb, :]
+
+            @pl.when(c == 0)
+            def _():
+                asw[0:nb, 0:nb] = jnp.where(sub <= lane, u_f[0:nb, 0:nb], 0.0)
+
+        @pl.when(r == 1)
+        def _():
+            asw[0:nb, :] = u_f[nb:two, :]
+
+            @pl.when(c == 0)
+            def _():
+                asw[0:nb, 0:nb] = res[1]
+
+            @pl.when(c == 1)
+            def _():
+                asw[0:nb, 0:nb] = jnp.where(sub <= lane, u_f[nb:two, 0:nb], 0.0)
 
     step = height // TILES
     tiles = [(t * step, step) for t in range(TILES - 1)]
     tiles += [(height - step, step // 2), (height - step // 2, step // 2)]
-    for start, count in tiles:
-        while left and left[0] * ck < start + count:
-            some(1)
+    for at, (start, count) in enumerate(tiles):
+        if at == LATE_TILE:
+            bring()
+            finish_top()
+        for queue in (left, late):
+            while any(k < CHUNKS and k * ck < start + count for k in queue):
+                step_on(queue, 1)
         for k in range(start // ck, (start + count) // ck):
             sib_in(k).wait_recv()
         update(start, count)
         some(1)
-        if start == 0:
-            @pl.when(r == 0)
-            def _():
-                asw[0:nb, :] = u_f[0:nb, :]
-
-                @pl.when(c == 0)
-                def _():
-                    asw[0:nb, 0:nb] = jnp.where(sub <= lane, u_f[0:nb, 0:nb], 0.0)
-
-            @pl.when(r == 1)
-            def _():
-                asw[0:nb, :] = u_f[nb:two, :]
-
-                @pl.when(c == 0)
-                def _():
-                    asw[0:nb, 0:nb] = res[1]
-
-                @pl.when(c == 1)
-                def _():
-                    asw[0:nb, 0:nb] = jnp.where(sub <= lane, u_f[nb:two, 0:nb], 0.0)
 
     for j in range(NJ):
         def gone(j=j):
@@ -631,7 +653,7 @@
             vm((cap * R, two), BF16), vm((nj, cap * R, nb), F32), vm((nj, 2 * cap * R, nb), F32),
             vm((2, 2 * cap * R, nb), F32), vm((nj, nb, nb), F32), vm((2, nb, nb), F32),
             vm((2, two, nb), F32), vm((2, height, nb), F32), vm((4, nb, nb), F32),
-            vm((two, two), BF16), vm((3 * two, two), BF16), vm((two, 6 * cap * R), BF16),
+            vm((3 * two, two), BF16), vm((two, 6 * cap * R), BF16),
             vm((3 * two, width), BF16), vm((two, width), BF16), vm((two, width), F32),
             vm((height, nb), F32),
             dma((nj,)), dma((R - 1,)), dma((2,)), dma((R - 1,)), dma((R - 1,)),

time: 34.4 us -> 32.4 us (0.942)
  Pallas kernels: 32 us -> 30 us
    pallas_call x1, Pallas kernels: 30.7 us -> 28.7 us  [even_device(): pl.pallas_call(functools.partial(kernel, R, C, nb), out_shape=jax.ShapeDt...]
where the time goes in v3:
time: 32.4 us; the launch traced here: 32.3 us
  Pallas kernels  30 us (93%)
  local copies, waits for them, and re-layouts  1.32 us (4%)
  between operations  0.67 us (2%)
    pallas_call x1, Pallas kernels, even_device(): pl.pallas_call(functools.partial(kernel, R, C, nb), out_shape=jax.ShapeDt...  28.7 us
    pallas_call x1, Pallas kernels, on_device(): pl.pallas_call(functools.partial(most_kernel, R, nb), out_shape=jax.Shape...  1.32 us
    unnamed x1, local copies, waits for them, and re-layouts  1.32 us

profile of v3, /device:TPU:25, one launch (start us, length us, event | category | flops | bytes accessed | tf_op | source)
XLA Modules:
  0.0 32.3 jit_solution(13885150022155897914)
XLA Ops:
  0.0 1.3 %shard_map.43 = s32[1]{0:T(128)} custom-call(s32[2,128]{1,0:T(2,128)} %piv_ref.1), custom_call_target="tpu_custom_call" | custom-call | tf_op jit(solution)/shard_map/pallas_call | solution.py:1038
  2.0 28.9 %conditional.1 = (f32[1024,512]{1,0:T(8,128)S(1)}) conditional(s32[]{:T(128)} %bitcast, (f32[1024,512]{1,0:T(8,128)}, s32[2,128]{1,0:T(2,128)}, f32[2,128,128]{2,1,0:T(8,128)}) %tuple.11, (f32[1024,512]{1,0:T(8,128)}, s32[2,128]{1,0:T(2,128)}, f32[2,128,128]{2,1,0:T(8,128)}) %tuple.11), branch_computations={%region_0.0_spmd, %region_1.0_spmd} | conditional | bytes 8 | solution.py:1044
  2.0 28.7 %branch_1_fun.1 = f32[1024,512]{1,0:T(8,128)S(1)} custom-call(f32[1024,512]{1,0:T(8,128)} %get-tuple-element.32.a_hbm, s32[2,128]{1,0:T(2,128)} %get-tuple-element.24.piv_ref, f32[2,128,128]{2,1,0:T(8,128)} %get-tuple-element.34.linv_ref), custom_call_target="tpu_custom_call" | custom-call | tf_op jit(solution)/shard_map/cond/branch_1_fun/pallas_call | solution.py:646
  30.9 1.3 %copy.13 = f32[1024,512]{1,0:T(8,128)} copy(f32[1024,512]{1,0:T(8,128)S(1)} %get-tuple-element.26) | data formatting | bytes 4194304

commit v4 on v3

--- a/solution.py
+++ b/solution.py
@@ -11,7 +11,7 @@
 F32 = jnp.float32
 BF16 = jnp.bfloat16
 CHUNKS = 16
-EARLY = 1
+EARLY = 0
 MIDDLE = 12
 ANY_EARLY = 3
 FAR = 4
@@ -271,16 +271,21 @@
     def root_copy(k):
         return remote(a_hbm.at[pl.ds(k * ck, ck), cols(0)], piece(k), ch_s.at[k], ch_r.at[k], after)
 
+    step = height // TILES
+    tiles = [(t * step, step) for t in range(TILES - 1)]
+    tiles += [(height - step, step // 2), (height - step // 2, step // 2)]
+    closing = {(start + count) // ck - 1: at for at, (start, count) in enumerate(tiles)}
+
     def spread(k, side):
         if k < CHUNKS:
-            return pan.at[side, pl.ds(k * ck, ck)]
+            return pan.at[side, pl.ds(*tiles[k])]
         return tpan.at[side, pl.ds(0, W)] if k == TQ else dall.at[side]
 
     def sib_copy(k):
         return remote(spread(k, s), spread(k, s), sb_s.at[k], sb_r.at[k], sibling)
 
     def root_sib(k):
-        return remote(a_hbm.at[pl.ds(k * ck, ck), cols(0)], spread(k, s), sb_s.at[k], sb_r.at[k], sibling)
+        return remote(a_hbm.at[pl.ds(*tiles[k]), cols(0)], spread(k, s), sb_s.at[k], sb_r.at[k], sibling)
 
     def sib_in(k):
         return remote(spread(k, 1 - s), spread(k, 1 - s), sb_s.at[k], sb_r.at[k], sibling)
@@ -294,8 +299,10 @@
             if k == DQ:
                 for off in range(1, R):
                     da_copy(off).start()
-            else:
-                sib_copy(k).start()
+            elif k == TQ:
+                sib_copy(TQ).start()
+            elif k in closing:
+                sib_copy(closing[k]).start()
 
     order = list(range(EARLY)) + [DQ] + list(range(EARLY, MIDDLE)) + [TQ] + list(range(MIDDLE, CHUNKS))
     left = order[:]
@@ -319,7 +326,8 @@
             @pl.when(has_after)
             def _():
                 root_copy(k).start()
-            root_sib(k).start()
+            if k in closing:
+                root_sib(closing[k]).start()
 
     @pl.when(at_root)
     def _():
@@ -466,18 +474,6 @@
         da_in(off).wait_recv()
     sib_copy(DQ).start()
 
-    @pl.when(at_root)
-    def _():
-        from_tops(tq_in)
-
-        @pl.when(has_after)
-        def _():
-            chain_copy(TQ).start()
-        sib_copy(TQ).start()
-        from_root(MIDDLE, CHUNKS)
-        tops[0] = tpan[s]
-        pall[0] = dall[s]
-
     step_on(left, INNER[3])
     step_on(late, LAST[3])
     sib_in(DQ).wait_recv()
@@ -492,6 +488,18 @@
     res[0] = quick_inverse(upper00, sub, lane, some)
     some(1)
     ag_pass(3)
+    @pl.when(at_root)
+    def _():
+        from_tops(tq_in)
+
+        @pl.when(has_after)
+        def _():
+            chain_copy(TQ).start()
+        sib_copy(TQ).start()
+        from_root(MIDDLE, CHUNKS)
+        tops[0] = tpan[s]
+        pall[0] = dall[s]
+
     res[1] = close(dh[0, nb:two, :], res[0])
     rest = dh[1, nb:two, :] - close(res[1], upper01)
     upper11 = jnp.where(sub <= lane, close(linv_ref[1], rest), 0.0)
@@ -595,9 +603,6 @@
             def _():
                 asw[0:nb, 0:nb] = jnp.where(sub <= lane, u_f[nb:two, 0:nb], 0.0)
 
-    step = height // TILES
-    tiles = [(t * step, step) for t in range(TILES - 1)]
-    tiles += [(height - step, step // 2), (height - step // 2, step // 2)]
     for at, (start, count) in enumerate(tiles):
         if at == LATE_TILE:
             bring()
@@ -605,8 +610,7 @@
         for queue in (left, late):
             while any(k < CHUNKS and k * ck < start + count for k in queue):
                 step_on(queue, 1)
-        for k in range(start // ck, (start + count) // ck):
-            sib_in(k).wait_recv()
+        sib_in(at).wait_recv()
         update(start, count)
         some(1)
 
@@ -625,9 +629,10 @@
     for off in range(1, R):
         da_copy(off).wait_send()
 
+    for k in list(range(len(tiles))) + [TQ, DQ]:
+        sib_copy(k).wait_send()
+
     for k in range(CHUNKS + 2):
-        sib_copy(k).wait_send()
-
         @pl.when(has_after)
         def _():
             chain_copy(k).wait_send()

time: 32.4 us -> 32.3 us (level)
  no operation moved by 1% of the time
where the time goes in v4:
time: 32.3 us; the launch traced here: 32.1 us
  Pallas kernels  29.9 us (93%)
  local copies, waits for them, and re-layouts  1.32 us (4%)
  between operations  0.67 us (2%)
    pallas_call x1, Pallas kernels, even_device(): pl.pallas_call(functools.partial(kernel, R, C, nb), out_shape=jax.ShapeDt...  28.6 us
    unnamed x1, local copies, waits for them, and re-layouts  1.32 us
    pallas_call x1, Pallas kernels, on_device(): pl.pallas_call(functools.partial(most_kernel, R, nb), out_shape=jax.Shape...  1.32 us

profile of v4, /device:TPU:25, one launch (start us, length us, event | category | flops | bytes accessed | tf_op | source)
XLA Modules:
  0.0 32.1 jit_solution(1324541738295786490)
XLA Ops:
  0.0 1.3 %shard_map.43 = s32[1]{0:T(128)} custom-call(s32[2,128]{1,0:T(2,128)} %piv_ref.1), custom_call_target="tpu_custom_call" | custom-call | tf_op jit(solution)/shard_map/pallas_call | solution.py:1043
  2.0 28.8 %conditional.1 = (f32[1024,512]{1,0:T(8,128)S(1)}) conditional(s32[]{:T(128)} %bitcast, (f32[1024,512]{1,0:T(8,128)}, s32[2,128]{1,0:T(2,128)}, f32[2,128,128]{2,1,0:T(8,128)}) %tuple.11, (f32[1024,512]{1,0:T(8,128)}, s32[2,128]{1,0:T(2,128)}, f32[2,128,128]{2,1,0:T(8,128)}) %tuple.11), branch_computations={%region_0.0_spmd, %region_1.0_spmd} | conditional | bytes 8 | solution.py:1049
  2.0 28.6 %branch_1_fun.1 = f32[1024,512]{1,0:T(8,128)S(1)} custom-call(f32[1024,512]{1,0:T(8,128)} %get-tuple-element.32.a_hbm, s32[2,128]{1,0:T(2,128)} %get-tuple-element.24.piv_ref, f32[2,128,128]{2,1,0:T(8,128)} %get-tuple-element.34.linv_ref), custom_call_target="tpu_custom_call" | custom-call | tf_op jit(solution)/shard_map/cond/branch_1_fun/pallas_call | solution.py:651
  30.8 1.3 %copy.13 = f32[1024,512]{1,0:T(8,128)} copy(f32[1024,512]{1,0:T(8,128)S(1)} %get-tuple-element.26) | data formatting | bytes 4194304
